TPU v7x, 32 devices: a whole 2x2x4 slice. The times are simulated.
32 devices in a mesh: group: 2 (over x), fsdp: 4 (over y, core), tensor: 4 (over z).
Axes of the slice: x: 2, y: 2, z: 4, core: 2. Of those that a mesh axis runs over, the one named last changes fastest.
Arguments:
- tokens: bfloat16 [2048, 4096], P(('group', 'fsdp'), 'tensor'), parts along dimension 0, may hold values from -6 to 6
- cotangent: bfloat16 [2048, 4096], P(('group', 'fsdp'), 'tensor'), parts along dimension 0, may hold values from -6 to 6
- gate_blocks: bfloat16 [4, 12, 128, 128], P('tensor', 'fsdp'), may hold values from -1 to 1
- up_blocks: bfloat16 [4, 12, 128, 128], P('tensor', 'fsdp'), may hold values from -1 to 1
- down_blocks: bfloat16 [4, 12, 128, 128], P('tensor', 'fsdp'), may hold values from -0.5 to 0.5
- block_rows: int32 [3, 4, 12], P(None, 'tensor'), may hold values from 0 to 31, as said below
- col_counts: int32 [3, 4, 28], P(None, 'tensor'), may hold values from 0 to 12, as said below
Outputs:
- layer_out: bfloat16 [2048, 4096], P(('group', 'fsdp'), 'tensor'), parts along dimension 0
- input_grad: bfloat16 [2048, 4096], P(('group', 'fsdp'), 'tensor'), parts along dimension 0
- gate_grad: bfloat16 [8, 12, 128, 128], P(('group', 'tensor'), 'fsdp'), parts along dimension 0
- up_grad: bfloat16 [8, 12, 128, 128], P(('group', 'tensor'), 'fsdp'), parts along dimension 0
- down_grad: bfloat16 [8, 12, 128, 128], P(('group', 'tensor'), 'fsdp'), parts along dimension 0
There are 2 independent parts, one for each index of `group`. A program takes and returns all parts, laid end to end along the dimension named above; an argument that names none is the same for every part. Nothing has to cross between parts.
Inputs may be any that keep to these rules, and one draw needn't show every extreme that they name: `block_rows`: for each matrix and tensor index, the live slots list their blocks column by column, feature blocks ascending within a column and no block twice; the entries past the live ones are 0. `col_counts`: for each matrix and tensor index the counts sum to half of 12 or more and to at most 12, and to exactly 12 at one tensor index of each matrix.
All inputs are finite; a program needn't handle non-finite values.
Results may differ from a plain program's by a relative error of at most 0.011.
Values may be sent and summed in bfloat16 or wider, within the bound.
A program may use at most 128 MiB of HBM per device.

v0:
```python
import jax
import jax.numpy as jnp
from jax import lax
from jax.sharding import PartitionSpec as P

finest = lax.Precision.HIGHEST


def slot_columns(counts, slot_count):
    running = jnp.cumsum(counts)
    places = lax.broadcasted_iota(jnp.int32, (slot_count, counts.shape[0]), 0)
    return jnp.sum((running[None, :] <= places).astype(jnp.int32), axis=1)


def slot_tables(slot_rows, counts, feature_count):
    slot_count = slot_rows.shape[0]
    col_width = counts.shape[0]
    columns = slot_columns(counts, slot_count)
    col_hot = (
        columns[:, None] == lax.broadcasted_iota(jnp.int32, (slot_count, col_width), 1)
    ).astype(jnp.float32)
    row_hot = (
        slot_rows[:, None] == lax.broadcasted_iota(jnp.int32, (slot_count, feature_count), 1)
    ).astype(jnp.float32)
    is_live = columns < col_width
    picker = jnp.minimum(columns, col_width - 1)
    return (col_hot, row_hot, is_live, picker)


def into_columns(terms, col_hot):
    return jnp.einsum("tsn,sc->tcn", terms, col_hot, precision=finest)


def into_rows(terms, row_hot):
    return jnp.einsum("tsk,sr->trk", terms, row_hot, precision=finest)


def pick_columns(values, picker, is_live):
    chosen = jnp.take(values, picker, axis=1)
    return jnp.where(is_live[None, :, None], chosen, jnp.zeros_like(chosen))


def on_device(tokens, cotangent, gate_blocks, up_blocks, down_blocks, block_rows, col_counts):
    full_tokens = lax.all_gather(tokens, "tensor", axis=1, tiled=True)
    gate_w, up_w = (
        lax.all_gather(gate_blocks[0], "fsdp", axis=0, tiled=True),
        lax.all_gather(up_blocks[0], "fsdp", axis=0, tiled=True),
    )
    slot_rows = block_rows[:, 0, :]
    counts = col_counts[:, 0, :]
    tok_count = full_tokens.shape[0]
    side = gate_w.shape[-1]
    feature_count = full_tokens.shape[1] // side
    token_blocks = full_tokens.reshape(tok_count, feature_count, side)
    gate_tab = slot_tables(slot_rows[0], counts[0], feature_count)
    up_tab = slot_tables(slot_rows[1], counts[1], feature_count)
    down_tab = slot_tables(slot_rows[2], counts[2], feature_count)
    gate_in = jnp.take(token_blocks, slot_rows[0], axis=1)
    up_in = jnp.take(token_blocks, slot_rows[1], axis=1)
    gate_pre = into_columns(
        jnp.einsum("tsk,skn->tsn", gate_in, gate_w, preferred_element_type=jnp.float32), gate_tab[0]
    )
    up_pre = into_columns(
        jnp.einsum("tsk,skn->tsn", up_in, up_w, preferred_element_type=jnp.float32), up_tab[0]
    )
    sigma_gate = jax.nn.sigmoid(gate_pre)
    active = gate_pre * sigma_gate
    hidden = (active * up_pre).astype(jnp.bfloat16)
    down_w = lax.all_gather(down_blocks[0], "fsdp", axis=0, tiled=True)
    down_in = pick_columns(hidden, down_tab[3], down_tab[2])
    out_terms = jnp.einsum("tsn,snk->tsk", down_in, down_w, preferred_element_type=jnp.float32)
    out_part = into_rows(out_terms, down_tab[1]).reshape(tok_count, -1)
    layer_out = lax.psum_scatter(
        out_part.astype(jnp.bfloat16), "tensor", scatter_dimension=1, tiled=True
    )
    full_grads = lax.all_gather(cotangent, "tensor", axis=1, tiled=True)
    grad_blocks = full_grads.reshape(tok_count, feature_count, side)
    down_back = jnp.take(grad_blocks, slot_rows[2], axis=1)
    down_part = jnp.einsum("tsn,tsk->snk", down_in, down_back, preferred_element_type=jnp.float32)
    back_terms = jnp.einsum("tsk,snk->tsn", down_back, down_w, preferred_element_type=jnp.float32)
    dhidden = into_columns(back_terms, down_tab[0])
    dgate = (dhidden * up_pre * sigma_gate * (1.0 + gate_pre * (1.0 - sigma_gate))).astype(
        jnp.bfloat16
    )
    dup = (dhidden * active).astype(jnp.bfloat16)
    gate_back = pick_columns(dgate, gate_tab[3], gate_tab[2])
    up_back = pick_columns(dup, up_tab[3], up_tab[2])
    gate_terms = jnp.einsum("tsn,skn->tsk", gate_back, gate_w, preferred_element_type=jnp.float32)
    up_terms = jnp.einsum("tsn,skn->tsk", up_back, up_w, preferred_element_type=jnp.float32)
    in_part = (into_rows(gate_terms, gate_tab[1]) + into_rows(up_terms, up_tab[1])).reshape(
        tok_count, -1
    )
    input_grad = lax.psum_scatter(
        in_part.astype(jnp.bfloat16), "tensor", scatter_dimension=1, tiled=True
    )
    gate_part = jnp.einsum("tsk,tsn->skn", gate_in, gate_back, preferred_element_type=jnp.float32)
    up_part = jnp.einsum("tsk,tsn->skn", up_in, up_back, preferred_element_type=jnp.float32)
    gate_sum, up_sum, down_sum = (
        lax.psum_scatter(
            gate_part.astype(jnp.bfloat16), "fsdp", scatter_dimension=0, tiled=True
        ).astype(jnp.float32),
        lax.psum_scatter(
            up_part.astype(jnp.bfloat16), "fsdp", scatter_dimension=0, tiled=True
        ).astype(jnp.float32),
        lax.psum_scatter(
            down_part.astype(jnp.bfloat16), "fsdp", scatter_dimension=0, tiled=True
        ).astype(jnp.float32),
    )
    gate_grad = gate_sum.astype(jnp.bfloat16)[None]
    up_grad = up_sum.astype(jnp.bfloat16)[None]
    down_grad = down_sum.astype(jnp.bfloat16)[None]
    return (layer_out, input_grad, gate_grad, up_grad, down_grad)


def solution(mesh):
    in_specs = (
        P(("group", "fsdp"), "tensor"),
        P(("group", "fsdp"), "tensor"),
        P("tensor", "fsdp", None, None),
        P("tensor", "fsdp", None, None),
        P("tensor", "fsdp", None, None),
        P(None, "tensor", None),
        P(None, "tensor", None),
    )
    out_specs = (
        P(("group", "fsdp"), "tensor"),
        P(("group", "fsdp"), "tensor"),
        P(("group", "tensor"), "fsdp", None, None),
        P(("group", "tensor"), "fsdp", None, None),
        P(("group", "tensor"), "fsdp", None, None),
    )
    return jax.shard_map(
        on_device, mesh=mesh, in_specs=in_specs, out_specs=out_specs, check_vma=False
    )
```

profile of v0, /device:TPU:0, one launch (start us, length us, event | category | flops | bytes accessed | tf_op | source)
XLA Modules:
  0.0 299.6 jit_solution(16463262677985737022)
XLA Ops:
  7.3 2.1 copy.95
  9.5 2.0 copy.107
  11.6 0.1 copy.100
  11.8 0.1 reduce.2
  11.9 0.1 copy.94
  12.0 0.1 reduce.1
  12.2 0.1 copy.93
  12.3 0.1 reduce
  12.5 0.1 convert_reduce_fusion.1
  12.6 0.1 convert_reduce_fusion
  12.7 0.1 convert_reduce_fusion.2
  12.9 8.4 %all-gather.1 = bf16[1,12,128,128]{3,2,0,1:T(8,128)(2,1)} all-gather(bf16[1,3,128,128]{3,2,0,1:T(8,128)(2,1)S(1)} %bitcast.155), channel_id=3, replica_groups=mesh['group'=2,'fsdp'=4,'tensor'=4] {'fsdp'}, dimensions={1}, use_global_device_ids=true | all-gather | bytes 491520 | tf_op jit(solution)/shard_map/all_gather | solution.py:47
  21.2 7.0 %all-gather = bf16[1,12,128,128]{3,2,0,1:T(8,128)(2,1)} all-gather(bf16[1,3,128,128]{3,2,0,1:T(8,128)(2,1)S(1)} %bitcast.156), channel_id=2, replica_groups=mesh['group'=2,'fsdp'=4,'tensor'=4] {'fsdp'}, dimensions={1}, use_global_device_ids=true | all-gather | bytes 491520 | tf_op jit(solution)/shard_map/all_gather | solution.py:46
  28.3 6.6 %all-gather.2 = bf16[1,12,128,128]{3,2,0,1:T(8,128)(2,1)S(1)} all-gather(bf16[1,3,128,128]{3,2,0,1:T(8,128)(2,1)S(1)} %bitcast.157), channel_id=4, replica_groups=mesh['group'=2,'fsdp'=4,'tensor'=4] {'fsdp'}, dimensions={1}, use_global_device_ids=true | all-gather | bytes 491520 | tf_op jit(solution)/shard_map/all_gather | solution.py:69
  34.8 24.0 %all-gather.6.cloned.1.call-done = bf16[256,4096]{0,1:T(8,128)(2,1)} async-done(((bf16[256,1024]{0,1:T(8,128)(2,1)}), bf16[256,4096]{0,1:T(8,128)(2,1)}) %all-gather.6.cloned.1.call-update) | async-done | bytes 2097168 | tf_op jit(solution)/shard_map/all_gather | solution.py:44
  58.9 3.2 %copy.96 = bf16[256,32,128]{2,0,1:T(8,128)(2,1)S(1)} copy(bf16[256,32,128]{0,2,1:T(8,128)(2,1)} %bitcast.154) | data formatting | bytes 4194304 | tf_op jit(solution)/shard_map/reshape | solution.py:54
  62.1 0.7 gather_fusion.1
  62.8 1.6 gather_fusion
  64.4 1.5 convolution_bitcast_fusion.4
  65.9 0.4 convolution_bitcast_fusion.5
  66.3 5.1 %fusion.16 = f32[28,256,128]{2,0,1:T(8,128)} fusion(f32[256,12,128]{2,0,1:T(8,128)S(1)} %convolution_bitcast_fusion.4, s32[12]{0:T(128)S(1)} %convert_reduce_fusion), kind=kOutput, calls=%fused_computation.31 | convolution fusion | flops 132120912 | bytes 5242928 | tf_op jit(solution)/shard_map/tsn,sc->tcn/dot_general | solution.py:31
  71.4 5.2 %fusion.18 = f32[28,256,128]{2,0,1:T(8,128)} fusion(f32[256,12,128]{2,0,1:T(8,128)S(1)} %convolution_bitcast_fusion.5, s32[12]{0:T(128)S(1)} %convert_reduce_fusion.1), kind=kOutput, calls=%fused_computation.33 | convolution fusion | flops 132120912 | bytes 5242928 | tf_op jit(solution)/shard_map/tsn,sc->tcn/dot_general | solution.py:31
  76.6 29.1 %all-gather.8.cloned.1.call-done = bf16[256,4096]{0,1:T(8,128)(2,1)} async-done(((bf16[256,1024]{0,1:T(8,128)(2,1)}), bf16[256,4096]{0,1:T(8,128)(2,1)}) %all-gather.8.cloned.1.call-update) | async-done | bytes 2097168 | tf_op jit(solution)/shard_map/all_gather | solution.py:76
  105.7 3.2 %copy.108 = bf16[256,32,128]{2,0,1:T(8,128)(2,1)S(1)} copy(bf16[256,32,128]{0,2,1:T(8,128)(2,1)} %bitcast.153) | data formatting | bytes 4194304 | tf_op jit(solution)/shard_map/reshape | solution.py:77
  108.9 1.6 gather_fusion.3
  110.5 1.7 convolution_bitcast_fusion.2
  112.2 2.6 fusion.12
  114.9 12.8 %fusion.3 = (bf16[256,28,128]{2,0,1:T(8,128)(2,1)}, bf16[256,28,128]{2,0,1:T(8,128)(2,1)}, bf16[256,28,128]{2,0,1:T(8,128)(2,1)S(1)}) fusion(f32[28,256,128]{2,0,1:T(8,128)S(1)} %fusion.12, f32[28,256,128]{2,0,1:T(8,128)S(1)} %copy-done.1, f32[28,256,128]{2,0,1:T(8,128)S(1)} %copy-done), kind=kLoop, calls=%fused_computation.12 | loop fusion | flops 13762560 | bytes 16515072 | tf_op jit(solution)/shard_map/convert_element_type | solution.py:85
  127.7 2.2 gather_fusion.4
  129.9 2.7 convolution_convert_fusion.2
  132.7 3.1 %gather_fusion.5 = bf16[12,256,128]{2,1,0:T(8,128)(2,1)} fusion(bf16[256,28,128]{2,0,1:T(8,128)(2,1)} %get-tuple-element.19, s32[1024]{0:T(1024)S(1)} %pad_clamp_fusion), kind=kCustom, calls=%fused_computation.5.clone | custom fusion | bytes 1572912 | tf_op jit(solution)/shard_map/jit(_take)/gather | solution.py:39
  135.8 2.4 convolution_convert_fusion.1
  138.3 0.7 gather_fusion.2
  139.0 0.4 copy-done.2
  139.4 1.3 convolution_convert_fusion
  140.7 1.4 convolution_bitcast_fusion.1
  142.1 1.7 convolution_bitcast_fusion
  143.8 2.7 fusion.10
  146.5 4.3 %add_convert_fusion = bf16[32,256,128]{2,0,1:T(8,128)(2,1)S(1)} fusion(f32[32,256,128]{2,0,1:T(8,128)S(1)} %fusion.10, f32[256,12,128]{2,0,1:T(8,128)S(1)} %convolution_bitcast_fusion, s32[12]{0:T(128)S(1)} %get-tuple-element.22), kind=kOutput, calls=%fused_computation.6 | convolution fusion | flops 153092480 | bytes 7864368 | tf_op jit(solution)/shard_map/tsk,sr->trk/dot_general | solution.py:35
  150.8 2.3 copy.147
  153.2 1.1 copy-done.6
  154.4 0.4 convolution_bitcast_fusion.3
  154.8 3.9 %fusion.20 = bf16[32,256,128]{2,0,1:T(8,128)(2,1)S(1)} fusion(f32[256,12,128]{2,0,1:T(8,128)S(1)} %convolution_bitcast_fusion.3, s32[12]{0:T(128)S(1)} %get-tuple-element.23), kind=kOutput, calls=%fused_computation.35 | convolution fusion | flops 152043904 | bytes 3670064 | tf_op jit(solution)/shard_map/tsk,sr->trk/dot_general | solution.py:35
  158.7 2.3 copy.148
  161.0 15.1 %reduce-scatter.12.cloned.1.call-done = bf16[3,128,128]{2,1,0:T(8,128)(2,1)} async-done(((bf16[12,128,128]{2,1,0:T(8,128)(2,1)}), bf16[3,128,128]{2,1,0:T(8,128)(2,1)}) %reduce-scatter.12.cloned.1.call-update) | async-done | bytes 98320 | tf_op jit(solution)/shard_map/reduce_scatter | solution.py:102
  176.1 23.8 %reduce-scatter.14.cloned.1.call-done = bf16[3,128,128]{2,1,0:T(8,128)(2,1)} async-done(((bf16[12,128,128]{2,1,0:T(8,128)(2,1)}), bf16[3,128,128]{2,1,0:T(8,128)(2,1)}) %reduce-scatter.14.cloned.1.call-update) | async-done | bytes 98320 | tf_op jit(solution)/shard_map/reduce_scatter | solution.py:105
  199.9 46.6 %reduce-scatter.8.cloned.1.call-done = bf16[256,1024]{1,0:T(8,128)(2,1)} async-done(((bf16[256,4096]{1,0:T(8,128)(2,1)}), bf16[256,1024]{1,0:T(8,128)(2,1)}) %reduce-scatter.8.cloned.1.call-update) | async-done | bytes 524304 | tf_op jit(solution)/shard_map/reduce_scatter | solution.py:93
  246.5 46.2 %reduce-scatter.6.cloned.1.call-done = bf16[256,1024]{1,0:T(8,128)(2,1)} async-done(((bf16[256,4096]{1,0:T(8,128)(2,1)}), bf16[256,1024]{1,0:T(8,128)(2,1)}) %reduce-scatter.6.cloned.1.call-update) | async-done | bytes 524304 | tf_op jit(solution)/shard_map/reduce_scatter | solution.py:73
  (60 shorter events, 0.8 us)
Async XLA Ops:
  7.2 4.4 %copy-start.14 = (s32[3,1,12]{2,1,0:T(1,128)S(1)}, s32[3,1,12]{2,1,0:T(1,128)}, u32[]{:S(2)}) copy-start(s32[3,1,12]{2,1,0:T(1,128)} %param.16) | copy-start | bytes 436
  7.2 4.4 %copy-start.15 = (s32[3,1,28]{2,1,0:T(1,128)S(1)}, s32[3,1,28]{2,1,0:T(1,128)}, u32[]{:S(2)}) copy-start(s32[3,1,28]{2,1,0:T(1,128)} %param.17) | copy-start | bytes 1012
  7.2 5.7 %copy-start.11 = (bf16[1,3,128,128]{3,2,1,0:T(8,128)(2,1)S(1)}, bf16[1,3,128,128]{3,2,1,0:T(8,128)(2,1)}, u32[]{:S(2)}) copy-start(bf16[1,3,128,128]{3,2,1,0:T(8,128)(2,1)} %param.14) | copy-start | bytes 294916
  7.2 14.1 %copy-start.12 = (bf16[1,3,128,128]{3,2,1,0:T(8,128)(2,1)S(1)}, bf16[1,3,128,128]{3,2,1,0:T(8,128)(2,1)}, u32[]{:S(2)}) copy-start(bf16[1,3,128,128]{3,2,1,0:T(8,128)(2,1)} %param.13) | copy-start | bytes 294916
  7.2 21.1 %copy-start.13 = (bf16[1,3,128,128]{3,2,1,0:T(8,128)(2,1)S(1)}, bf16[1,3,128,128]{3,2,1,0:T(8,128)(2,1)}, u32[]{:S(2)}) copy-start(bf16[1,3,128,128]{3,2,1,0:T(8,128)(2,1)} %param.15) | copy-start | bytes 294916
  7.2 51.6 %all-gather.6.cloned.1.call-start = ((), (), s32[]{:S(2)}) async-start(), calls=%async_computation.5 | async-start | bytes 2621440 | tf_op jit(solution)/shard_map/all_gather | solution.py:44
  9.4 96.3 %all-gather.8.cloned.1.call-start = ((), (), s32[]{:S(2)}) async-start(), calls=%async_computation.7 | async-start | bytes 2621440 | tf_op jit(solution)/shard_map/all_gather | solution.py:76
  11.5 149.5 %reduce-scatter.10.cloned.1.call-start = ((), (), s32[]{:S(2)}) async-start(), calls=%async_computation.9 | async-start | bytes 491520 | tf_op jit(solution)/shard_map/reduce_scatter | solution.py:99
  34.8 75.7 %copy-start.8 = (bf16[1,12,128,128]{3,2,0,1:T(8,128)(2,1)}, bf16[1,12,128,128]{3,2,0,1:T(8,128)(2,1)S(1)}, u32[]{:S(2)}) copy-start(bf16[1,12,128,128]{3,2,0,1:T(8,128)(2,1)S(1)} %all-gather.2) | copy-start | bytes 1179652
  64.4 1.5 copy-start.7
  64.4 1.5 copy-start.10
  110.5 4.4 %copy-start.1 = (f32[28,256,128]{2,0,1:T(8,128)S(1)}, f32[28,256,128]{2,0,1:T(8,128)}, u32[]{:S(2)}) copy-start(f32[28,256,128]{2,0,1:T(8,128)} %fusion.18) | copy-start | bytes 11010052
  112.2 2.7 copy-start
  129.9 5.9 %copy-start.3 = (bf16[12,256,128]{2,1,0:T(8,128)(2,1)}, bf16[12,256,128]{2,1,0:T(8,128)(2,1)S(1)}, u32[]{:S(2)}) copy-start(bf16[12,256,128]{2,1,0:T(8,128)(2,1)S(1)} %gather_fusion.4) | copy-start | bytes 2359300
  132.6 43.5 %reduce-scatter.12.cloned.1.call-start = ((), (), s32[]{:S(2)}) async-start(), calls=%async_computation.10 | async-start | bytes 491520 | tf_op jit(solution)/shard_map/reduce_scatter | solution.py:102
  138.2 1.2 copy-start.2
  138.3 61.7 %reduce-scatter.14.cloned.1.call-start = ((), (), s32[]{:S(2)}) async-start(), calls=%async_computation.11 | async-start | bytes 491520 | tf_op jit(solution)/shard_map/reduce_scatter | solution.py:105
  139.0 1.6 copy-start.5
  139.0 1.6 copy-start.4
  143.8 102.8 %reduce-scatter.8.cloned.1.call-start = ((), (), s32[]{:S(2)}) async-start(), calls=%async_computation.8 | async-start | bytes 2621440 | tf_op jit(solution)/shard_map/reduce_scatter | solution.py:93
  153.1 1.1 copy-start.6
  153.1 1.2 copy-start.9
  153.2 139.6 %reduce-scatter.6.cloned.1.call-start = ((), (), s32[]{:S(2)}) async-start(), calls=%async_computation.6 | async-start | bytes 2621440 | tf_op jit(solution)/shard_map/reduce_scatter | solution.py:73
Sparse Core Ops, SparseCore 0:
  10.2 48.6 all-gather.5
  61.0 44.6 all-gather.7
  132.8 19.5 reduce-scatter.9
  155.3 20.8 reduce-scatter.11
  179.0 20.8 reduce-scatter.13
  202.6 43.8 reduce-scatter.7
  249.5 43.1 reduce-scatter.5
where the time goes:
time: 300 us
  waiting for transfers between devices  185 us (62%)
  matrix products  37.3 us (12%)
  local copies, waits for them, and re-layouts  26.9 us (9%)
  blocking collectives  22 us (7%)
  between operations  14.5 us (5%)
  other arithmetic  13.8 us (5%)
    reduce_scatter x1, waiting for transfers between devices, on_device(): lax.psum_scatter(in_part.astype(jnp.bfloat16), 'tensor', scatter_dimensio...  46.6 us
    reduce_scatter x1, waiting for transfers between devices, on_device(): lax.psum_scatter(out_part.astype(jnp.bfloat16), 'tensor', scatter_dimensi...  46.2 us
    all_gather x1, waiting for transfers between devices, on_device(): full_grads = lax.all_gather(cotangent, 'tensor', axis=1, tiled=True)  29.1 us
    all_gather x1, waiting for transfers between devices, on_device(): full_tokens = lax.all_gather(tokens, 'tensor', axis=1, tiled=True)  24 us
    reduce_scatter x1, waiting for transfers between devices, on_device(): lax.psum_scatter(down_part.astype(jnp.bfloat16), 'fsdp', scatter_dimensio...  23.8 us
    reduce_scatter x1, waiting for transfers between devices, on_device(): lax.psum_scatter(up_part.astype(jnp.bfloat16), 'fsdp', scatter_dimension=...  15.1 us
    dot_general x3, matrix products, into_columns(): return jnp.einsum('tsn,sc->tcn', terms, col_hot, precision=finest)  12.9 us
    convert_element_type x1, other arithmetic, on_device(): dup = (dhidden * active).astype(jnp.bfloat16)  12.8 us
  transfers between devices with their start and end apart: 7, of which 6 were waited for; matrix products, arithmetic and copies ran while one was open for 16% of the time, Pallas kernels for 0%

commit v1 on v0

--- a/solution.py
+++ b/solution.py
@@ -1,6 +1,10 @@
+import functools
+
 import jax
 import jax.numpy as jnp
 from jax import lax
+from jax.experimental import pallas as pl
+from jax.experimental.pallas import tpu as pltpu
 from jax.sharding import PartitionSpec as P
 
 finest = lax.Precision.HIGHEST
@@ -40,7 +44,7 @@
     return jnp.where(is_live[None, :, None], chosen, jnp.zeros_like(chosen))
 
 
-def on_device(tokens, cotangent, gate_blocks, up_blocks, down_blocks, block_rows, col_counts):
+def gathered_plan(tokens, cotangent, gate_blocks, up_blocks, down_blocks, block_rows, col_counts):
     full_tokens = lax.all_gather(tokens, "tensor", axis=1, tiled=True)
     gate_w, up_w = (
         lax.all_gather(gate_blocks[0], "fsdp", axis=0, tiled=True),
@@ -112,7 +116,144 @@
     return (layer_out, input_grad, gate_grad, up_grad, down_grad)
 
 
+def block_pass(slots, width, shares, meta_ref, acts_ref, w_ref, y_ref, g_ref, gate, up, dhid, hid, dgate, dup, acc):
+    n_tensor, tok, feats = acts_ref.shape[1:]
+    side = w_ref.shape[-1]
+    per_chunk = feats // side
+    per_share = slots // shares
+    trash, zero = width, width + 1
+
+    def row_of(t, m, s):
+        return meta_ref[t * 6 * slots + m * 2 * slots + s]
+
+    def col_of(t, m, s, dead):
+        col = meta_ref[t * 6 * slots + m * 2 * slots + slots + s]
+        return jnp.where(col < width, col, dead)
+
+    def act(which, row):
+        lanes = pl.ds(pl.multiple_of(lax.rem(row, per_chunk) * side, side), side)
+        return acts_ref[which, lax.div(row, per_chunk), :, lanes]
+
+    def place(t, m, s):
+        share, k = divmod(s, per_share)
+        return share * n_tensor + t, pl.ds((m * per_share + k) * side, side)
+
+    def weight(t, m, s):
+        unit, rows = place(t, m, s)
+        return w_ref[unit, rows, :]
+
+    def dot(a, b, dims):
+        return lax.dot_general(a, b, (dims, ((), ())), preferred_element_type=jnp.float32)
+
+    plain, right_t, left_t = ((1,), (0,)), ((1,), (1,)), ((0,), (0,))
+    acc[...] = jnp.zeros_like(acc)
+
+    @pl.loop(0, n_tensor)
+    def _(t):
+        gate[...] = jnp.zeros_like(gate)
+        up[...] = jnp.zeros_like(up)
+        dhid[...] = jnp.zeros_like(dhid)
+        for m, which, dims, into in ((0, 0, plain, gate), (1, 0, plain, up), (2, 1, right_t, dhid)):
+            terms = [dot(act(which, row_of(t, m, s)), weight(t, m, s), dims) for s in range(slots)]
+            for s in range(slots):
+                into[col_of(t, m, s, trash)] += terms[s]
+
+        @pl.loop(0, width)
+        def _(c):
+            g, u, d = gate[c], up[c], dhid[c]
+            sig = jax.nn.sigmoid(g)
+            active = g * sig
+            hid[c] = (active * u).astype(hid.dtype)
+            dgate[c] = (d * u * sig * (1.0 + g * (1.0 - sig))).astype(dgate.dtype)
+            dup[c] = (d * active).astype(dup.dtype)
+
+        for ref in (hid, dgate, dup):
+            ref[zero] = jnp.zeros_like(ref[zero])
+
+        for m, which, vals, dims, out in ((2, 1, hid, plain, 0), (0, 0, dgate, right_t, 1), (1, 0, dup, right_t, 1)):
+            rows = [row_of(t, m, s) for s in range(slots)]
+            picked = [vals[col_of(t, m, s, zero)] for s in range(slots)]
+            terms = [dot(picked[s], weight(t, m, s), dims) for s in range(slots)]
+            for s in range(slots):
+                unit, at = place(t, m, s)
+                other = act(which, rows[s])
+                pair = (picked[s], other) if m == 2 else (other, picked[s])
+                g_ref[unit, at, :] = dot(*pair, left_t).astype(g_ref.dtype)
+            for s in range(slots):
+                acc[out, rows[s]] += terms[s]
+
+    for out in range(2):
+        for chunk in range(n_tensor):
+            for j in range(per_chunk):
+                y_ref[out, chunk, :, pl.ds(j * side, side)] = acc[out, chunk * per_chunk + j].astype(y_ref.dtype)
+
+
+def run_blocks(meta, acts, weights, slots, width, shares):
+    n_tensor, tok, feats = acts.shape[1:]
+    units, _, side = weights.shape
+    vmem = pl.BlockSpec(memory_space=pltpu.VMEM)
+    cols = (width + 2, tok, side)
+    return pl.pallas_call(
+        functools.partial(block_pass, slots, width, shares),
+        out_shape=(
+            jax.ShapeDtypeStruct(acts.shape, acts.dtype),
+            jax.ShapeDtypeStruct((units, 3 * slots // shares * side, side), weights.dtype),
+        ),
+        in_specs=[pl.BlockSpec(memory_space=pltpu.SMEM), vmem, vmem],
+        out_specs=(vmem, vmem),
+        scratch_shapes=[pltpu.VMEM(cols, jnp.float32)] * 3
+        + [pltpu.VMEM(cols, jnp.bfloat16)] * 3
+        + [pltpu.VMEM((2, n_tensor * feats // side, tok, side), jnp.float32)],
+        compiler_params=pltpu.CompilerParams(vmem_limit_bytes=48 * 1024 * 1024),
+    )(meta, acts, weights)
+
+
+def pack_unit(gate_blocks, up_blocks, down_blocks, block_rows, col_counts):
+    slots = block_rows.shape[-1]
+    side = gate_blocks.shape[-1]
+    cols = jax.vmap(lambda c: slot_columns(c, slots))(col_counts[:, 0, :])
+    table = jnp.concatenate([block_rows[:, 0, :], cols], axis=1).reshape(-1)
+    table = jnp.pad(table, (0, 16 * side - table.shape[0])).reshape(16, side)
+    blocks = [b[0].reshape(-1, side) for b in (gate_blocks, up_blocks, down_blocks)]
+    return jnp.concatenate(blocks + [table.astype(jnp.bfloat16)], axis=0)
+
+
+def spread_plan(n_fsdp, n_tensor, tokens, cotangent, gate_blocks, up_blocks, down_blocks, block_rows, col_counts):
+    slots, width = block_rows.shape[-1], col_counts.shape[-1]
+    tok_count, feats = tokens.shape
+    side = gate_blocks.shape[-1]
+    per_share = slots // n_fsdp
+    unit = pack_unit(gate_blocks, up_blocks, down_blocks, block_rows, col_counts)
+    acts = jnp.stack([tokens, cotangent]).reshape(2, n_tensor, tok_count // n_tensor, feats)
+    weights, acts = bring(n_fsdp, n_tensor, unit, acts)
+    meta = weights[:n_tensor, -16:, :].astype(jnp.int32).reshape(n_tensor, -1)
+    meta = meta[:, : 6 * slots].reshape(-1)
+    y, grads = run_blocks(meta, acts, weights, slots, width, n_fsdp)
+    y, own = send_back(n_fsdp, n_tensor, y, grads)
+    y = y.reshape(2, tok_count, feats)
+    own = own.reshape(3, 1, per_share, side, side)
+    return y[0], y[1], own[0], own[1], own[2]
+
+
+def bring(n_fsdp, n_tensor, unit, acts):
+    weights = lax.all_gather(unit, ("fsdp", "tensor"), axis=0)
+    return weights, lax.all_to_all(acts, "tensor", 1, 1, tiled=True)
+
+
+def send_back(n_fsdp, n_tensor, y, grads):
+    own = lax.psum_scatter(grads, ("fsdp", "tensor"), scatter_dimension=0, tiled=True)
+    return lax.all_to_all(y, "tensor", 1, 1, tiled=True), own[0]
+
+
 def solution(mesh):
+    n_fsdp, n_tensor = mesh.shape["fsdp"], mesh.shape["tensor"]
+
+    def on_device(*args):
+        block_bytes = 3 * args[2].size * args[2].dtype.itemsize * n_fsdp * n_tensor
+        if block_bytes <= 8 * 1024 * 1024 and args[0].shape[0] % (16 * n_tensor) == 0:
+            return spread_plan(n_fsdp, n_tensor, *args)
+        return gathered_plan(*args)
+
     in_specs = (
         P(("group", "fsdp"), "tensor"),
         P(("group", "fsdp"), "tensor"),

time: 300 us -> 178 us (0.59)
  waiting for transfers between devices: 185 us -> 70.4 us
  blocking collectives: 22 us -> 70.6 us
  matrix products: 37.3 us -> 0 us
  local copies, waits for them, and re-layouts: 26.9 us -> 4.51 us
  Pallas kernels: 0 us -> 14.3 us
  other arithmetic: 13.8 us -> 4.16 us
    reduce_scatter x5 -> x1, waiting for transfers between devices: 132 us -> 44 us  [send_back(): lax.psum_scatter(grads, ('fsdp', 'tensor'), scatter_dimension=0, tiled=True)]
    all_to_all x0 -> x2, blocking collectives: none -> 70.6 us  [the longest x1 41.5 us: bring(): return (weights, lax.all_to_all(acts, 'tensor', 1, 1, tiled=True))]
    dot_general x15 -> x0, matrix products: 37.3 us -> none  [the longest x3 12.9 us: into_columns(): return jnp.einsum('tsn,sc->tcn', terms, col_hot, precision=finest)]
    all_gather x2 -> x1, waiting for transfers between devices: 53.1 us -> 26.4 us  [bring(): weights = lax.all_gather(unit, ('fsdp', 'tensor'), axis=0)]
    all_gather x3 -> x0, blocking collectives: 22 us -> none  [the longest x1 8.38 us: on_device(): lax.all_gather(up_blocks[0], 'fsdp', axis=0, tiled=True)]
    pallas_call x0 -> x1, Pallas kernels: none -> 14.3 us  [run_blocks(): pl.pallas_call(functools.partial(block_pass, slots, width, shares), out_s...]
    convert_element_type x1 -> x0, other arithmetic: 12.8 us -> none  [on_device(): dup = (dhidden * active).astype(jnp.bfloat16)]
    gather x6 -> x0, local copies, waits for them, and re-layouts: 9.81 us -> none  [the longest x3 5.95 us: pick_columns(): chosen = jnp.take(values, picker, axis=1)]
  transfers between devices with their start and end apart: 7 -> 2, of which waited for: 6 -> 2; matrix products, arithmetic and copies ran while one was open for 16% -> 1% of each run, Pallas kernels for 0% -> 0%
where the time goes in v1:
time: 178 us
  blocking collectives  70.6 us (40%)
  waiting for transfers between devices  70.4 us (40%)
  Pallas kernels  14.3 us (8%)
  between operations  14.1 us (8%)
  local copies, waits for them, and re-layouts  4.51 us (3%)
  other arithmetic  4.16 us (2%)
    reduce_scatter x1, waiting for transfers between devices, send_back(): lax.psum_scatter(grads, ('fsdp', 'tensor'), scatter_dimension=0, tiled=True)  44 us
    all_to_all x1, blocking collectives, bring(): return (weights, lax.all_to_all(acts, 'tensor', 1, 1, tiled=True))  41.5 us
    all_to_all x1, blocking collectives, send_back(): return (lax.all_to_all(y, 'tensor', 1, 1, tiled=True), own[0])  29.1 us
    all_gather x1, waiting for transfers between devices, bring(): weights = lax.all_gather(unit, ('fsdp', 'tensor'), axis=0)  26.4 us
    pallas_call x1, Pallas kernels, run_blocks(): pl.pallas_call(functools.partial(block_pass, slots, width, shares), out_s...  14.3 us
  transfers between devices with their start and end apart: 2, of which 2 were waited for; matrix products, arithmetic and copies ran while one was open for 1% of the time, Pallas kernels for 0%

profile of v1, /device:TPU:0, one launch (start us, length us, event | category | flops | bytes accessed | tf_op | source)
XLA Modules:
  0.0 178.0 jit_solution(3864448360500976878)
XLA Ops:
  7.2 0.0 all-gather.3.cloned.1.call-start
  7.2 0.7 convert.13
  7.9 0.7 copy.23
  8.6 0.2 reduce_window_sum.14
  8.8 0.1 convert_reduce_fusion
  8.9 0.1 pad_maximum_fusion.2
  9.0 0.1 reshape.44
  9.1 1.7 pad_maximum_fusion.1
  10.9 0.0 all-gather.3.cloned.1.call-update
  10.9 0.0 reduce-scatter.2.cloned.1.call-start
  10.9 1.3 pad_maximum_fusion
  12.2 41.5 %all_to_all.10 = bf16[2,4,64,1024]{3,2,0,1:T(8,128)(2,1)S(1)} all-to-all(bf16[2,4,64,1024]{3,2,0,1:T(8,128)(2,1)S(1)} %pad_maximum_fusion), channel_id=1, replica_groups=mesh['group'=2,'fsdp'=4,'tensor'=4] {'tensor'}, dimensions={1} | all-to-all | bytes 2097152 | tf_op jit(solution)/shard_map/all_to_all | solution.py:240
  53.7 0.1 copy.14.acts_ref
  53.8 26.4 %all-gather.3.cloned.1.call-done = bf16[18688,128]{1,0:T(8,128)(2,1)} async-done(((bf16[1168,128]{1,0:T(8,128)(2,1)}), bf16[18688,128]{1,0:T(8,128)(2,1)}) %all-gather.3.cloned.1.call-update) | async-done | bytes 4784144 | tf_op jit(solution)/shard_map/all_gather | solution.py:239
  80.1 0.7 slice_bitcast_fusion
  80.9 0.1 reshape.49.meta_ref
  81.0 14.3 %shard_map.110 = (bf16[2,4,64,1024]{3,2,1,0:T(8,128)(2,1)S(1)}, bf16[16,1152,128]{2,1,0:T(8,128)(2,1)}) custom-call(s32[288]{0:T(512)S(1)} %reshape.49.meta_ref, bf16[2,4,64,1024]{3,2,1,0:T(8,128)(2,1)S(1)} %copy.14.acts_ref, bf16[16,1168,128]{2,1,0:T(8,128)(2,1)} %bitcast.25), custom_call_target="tpu_custom_call" | custom-call | tf_op jit(solution)/shard_map/pallas_call | solution.py:196
  95.2 0.0 reduce-scatter.2.cloned.1.call-update
  95.3 0.1 copy.15
  95.3 29.1 %all_to_all.11 = bf16[2,4,64,1024]{3,2,0,1:T(8,128)(2,1)S(1)} all-to-all(bf16[2,4,64,1024]{3,2,0,1:T(8,128)(2,1)S(1)} %copy.15), channel_id=1, replica_groups=mesh['group'=2,'fsdp'=4,'tensor'=4] {'tensor'}, dimensions={1} | all-to-all | bytes 2097152 | tf_op jit(solution)/shard_map/all_to_all | solution.py:245
  124.4 1.1 fusion
  125.5 44.0 %reduce-scatter.2.cloned.1.call-done = bf16[1,1152,128]{2,1,0:T(8,128)(2,1)} async-done(((bf16[16,1152,128]{2,1,0:T(8,128)(2,1)}), bf16[1,1152,128]{2,1,0:T(8,128)(2,1)}) %reduce-scatter.2.cloned.1.call-update) | async-done | bytes 294928 | tf_op jit(solution)/shard_map/reduce_scatter | solution.py:244
  169.5 1.7 fusion.1
  (5 shorter events, 0.0 us)
Async XLA Ops:
  7.2 73.0 %all-gather.3.cloned.1.call-start = ((), (), s32[]{:S(2)}) async-start(), calls=%async_computation.4 | async-start | bytes 5083136 | tf_op jit(solution)/shard_map/all_gather | solution.py:239
  10.9 158.6 %reduce-scatter.2.cloned.1.call-start = ((), (), s32[]{:S(2)}) async-start(), calls=%async_computation.3 | async-start | bytes 5013504 | tf_op jit(solution)/shard_map/reduce_scatter | solution.py:244
Sparse Core Ops, SparseCore 0:
  11.0 69.0 all-gather.2
  95.4 74.0 reduce-scatter.1

commit v2 on v1

--- a/solution.py
+++ b/solution.py
@@ -213,36 +213,243 @@
     side = gate_blocks.shape[-1]
     cols = jax.vmap(lambda c: slot_columns(c, slots))(col_counts[:, 0, :])
     table = jnp.concatenate([block_rows[:, 0, :], cols], axis=1).reshape(-1)
-    table = jnp.pad(table, (0, 16 * side - table.shape[0])).reshape(16, side)
+    table = jnp.pad(table, (0, 32 * side - table.shape[0])).reshape(32, side)
     blocks = [b[0].reshape(-1, side) for b in (gate_blocks, up_blocks, down_blocks)]
     return jnp.concatenate(blocks + [table.astype(jnp.bfloat16)], axis=0)
 
 
 def spread_plan(n_fsdp, n_tensor, tokens, cotangent, gate_blocks, up_blocks, down_blocks, block_rows, col_counts):
     slots, width = block_rows.shape[-1], col_counts.shape[-1]
-    tok_count, feats = tokens.shape
-    side = gate_blocks.shape[-1]
-    per_share = slots // n_fsdp
     unit = pack_unit(gate_blocks, up_blocks, down_blocks, block_rows, col_counts)
-    acts = jnp.stack([tokens, cotangent]).reshape(2, n_tensor, tok_count // n_tensor, feats)
-    weights, acts = bring(n_fsdp, n_tensor, unit, acts)
-    meta = weights[:n_tensor, -16:, :].astype(jnp.int32).reshape(n_tensor, -1)
+    weights, acts = bring(n_fsdp, n_tensor, unit, tokens, cotangent)
+    meta = weights[:n_tensor, -32:, :].astype(jnp.int32).reshape(n_tensor, -1)
     meta = meta[:, : 6 * slots].reshape(-1)
     y, grads = run_blocks(meta, acts, weights, slots, width, n_fsdp)
-    y, own = send_back(n_fsdp, n_tensor, y, grads)
-    y = y.reshape(2, tok_count, feats)
-    own = own.reshape(3, 1, per_share, side, side)
-    return y[0], y[1], own[0], own[1], own[2]
-
-
-def bring(n_fsdp, n_tensor, unit, acts):
-    weights = lax.all_gather(unit, ("fsdp", "tensor"), axis=0)
-    return weights, lax.all_to_all(acts, "tensor", 1, 1, tiled=True)
+    return send_back(n_fsdp, n_tensor, y, grads)
+
+
+def greet(peers):
+    barrier = pltpu.get_barrier_semaphore()
+    for peer in peers:
+        pl.semaphore_signal(barrier, inc=1, device_id=peer, device_id_type=pl.DeviceIdType.MESH)
+    pl.semaphore_wait(barrier, len(peers))
+
+
+def remote(src, dst, send_sem, recv_sem, peer):
+    return pltpu.make_async_remote_copy(
+        src_ref=src, dst_ref=dst, send_sem=send_sem, recv_sem=recv_sem,
+        device_id=peer, device_id_type=pl.DeviceIdType.MESH,
+    )
+
+
+def bring_kernel(
+    n_tensor, unit_ref, tok_ref, cot_ref, w_ref, acts_ref,
+    z_send, y_send, x_send, c_send, a_send, z_recv, y_recv, x_recv, c_recv, a_recv, own_sem,
+):
+    group, f, t = (lax.axis_index(a) for a in ("group", "fsdp", "tensor"))
+    f_core = f + 1 - 2 * lax.rem(f, 2)
+    f_y = lax.rem(f + 2, 4)
+    f_diag = f_core + f_y - f
+    x_peer, y_peer, c_peer = {"group": 1 - group}, {"fsdp": f_y}, {"fsdp": f_core}
+    others = [lax.rem(t + d, n_tensor) for d in range(1, n_tensor)]
+    greet([{"tensor": o} for o in others] + [x_peer, y_peer, c_peer])
+
+    half = unit_ref.shape[0] // 2
+    mine = pl.ds(pl.multiple_of(group * half, 16), half)
+    theirs = pl.ds(pl.multiple_of((1 - group) * half, 16), half)
+    rows = tok_ref.shape[0] // n_tensor
+
+    def at(ff, tt):
+        return ff * n_tensor + tt
+
+    def chunk(tt):
+        return pl.ds(pl.multiple_of(tt * rows, 16), rows)
+
+    sends = []
+
+    def go(copy):
+        copy.start()
+        sends.append(copy)
+
+    def arrived(view, sem):
+        remote(view, view, own_sem.at[0], sem, c_peer).wait_recv()
+
+    me = at(f, t)
+    for d, o in enumerate(others):
+        go(remote(unit_ref.at[mine], w_ref.at[me, mine], z_send.at[d], z_recv.at[t], {"tensor": o}))
+    go(remote(unit_ref.at[mine], w_ref.at[me, mine], y_send.at[n_tensor - 1], y_recv.at[t], y_peer))
+    go(remote(unit_ref, w_ref.at[me], c_send.at[0], c_recv.at[at(0, t)], c_peer))
+    locals_ = [pltpu.make_async_copy(unit_ref, w_ref.at[me], own_sem.at[1])]
+    for i, ref in enumerate((tok_ref, cot_ref)):
+        locals_.append(pltpu.make_async_copy(ref.at[chunk(t)], acts_ref.at[i, t], own_sem.at[2 + i]))
+    for copy in locals_:
+        copy.start()
+
+    arrived(w_ref.at[at(f_y, t), mine], y_recv.at[t])
+    part = w_ref.at[at(f_y, t), mine]
+    go(remote(part, part, x_send.at[0], x_recv.at[at(1, t)], x_peer))
+    for d, o in enumerate(others):
+        part = w_ref.at[at(f, o), mine]
+        arrived(part, z_recv.at[o])
+        go(remote(part, part, y_send.at[d], y_recv.at[o], y_peer))
+        go(remote(part, part, x_send.at[1 + d], x_recv.at[at(0, o)], x_peer))
+    for d, o in enumerate(others):
+        for i, ref in enumerate((tok_ref, cot_ref)):
+            go(remote(ref.at[chunk(o)], acts_ref.at[i, t], a_send.at[2 * d + i], a_recv.at[2 * t + i], {"tensor": o}))
+    for d, o in enumerate(others):
+        part = w_ref.at[at(f_y, o), mine]
+        arrived(part, y_recv.at[o])
+        go(remote(part, part, x_send.at[n_tensor + d], x_recv.at[at(1, o)], x_peer))
+    part = w_ref.at[at(f_y, t)]
+    arrived(w_ref.at[at(f_y, t), theirs], x_recv.at[at(1, t)])
+    go(remote(part, part, c_send.at[1], c_recv.at[at(1, t)], c_peer))
+    for k, ff in enumerate((f, f_y)):
+        for d, o in enumerate(others):
+            part = w_ref.at[at(ff, o)]
+            arrived(w_ref.at[at(ff, o), theirs], x_recv.at[at(k, o)])
+            go(remote(part, part, c_send.at[2 + k * (n_tensor - 1) + d], c_recv.at[at(k, o)], c_peer))
+    for k, ff in enumerate((f_core, f_diag)):
+        for o in [t] + others:
+            arrived(w_ref.at[at(ff, o)], c_recv.at[at(k, o)])
+    for o in others:
+        for i in range(2):
+            arrived(acts_ref.at[i, o], a_recv.at[2 * o + i])
+    for copy in locals_:
+        copy.wait()
+    for copy in sends:
+        copy.wait_send()
+
+
+def bring(n_fsdp, n_tensor, unit, tokens, cotangent):
+    tok_count, feats = tokens.shape
+    anywhere = pl.BlockSpec(memory_space=pl.ANY)
+    sem = pltpu.SemaphoreType.DMA
+    return pl.pallas_call(
+        functools.partial(bring_kernel, n_tensor),
+        out_shape=(
+            jax.ShapeDtypeStruct((n_fsdp * n_tensor,) + unit.shape, unit.dtype),
+            jax.ShapeDtypeStruct((2, n_tensor, tok_count // n_tensor, feats), tokens.dtype),
+        ),
+        in_specs=[anywhere] * 3,
+        out_specs=(anywhere,) * 2,
+        scratch_shapes=[
+            sem((n_tensor - 1,)), sem((n_tensor,)), sem((2 * n_tensor - 1,)), sem((2 * n_tensor,)), sem((2 * n_tensor - 2,)),
+            sem((n_tensor,)), sem((n_tensor,)), sem((2 * n_tensor,)), sem((2 * n_tensor,)), sem((2 * n_tensor,)), sem((4,)),
+        ],
+        compiler_params=pltpu.CompilerParams(collective_id=0, has_side_effects=True),
+    )(unit, tokens, cotangent)
+
+
+def return_kernel(
+    n_tensor, y_ref, g_ref, out_ref, back_ref, gate_ref, up_ref, down_ref,
+    c_buf, y_out, y_buf, z_out, z_buf, c_send, y_send, z_send, a_send, c_recv, y_recv, z_recv, a_recv, own_sem,
+):
+    f, t = lax.axis_index("fsdp"), lax.axis_index("tensor")
+    f_core = f + 1 - 2 * lax.rem(f, 2)
+    f_y = lax.rem(f + 2, 4)
+    f_diag = f_core + f_y - f
+    y_peer, c_peer = {"fsdp": f_y}, {"fsdp": f_core}
+    others = [lax.rem(t + d, n_tensor) for d in range(1, n_tensor)]
+    greet([{"tensor": o} for o in others] + [y_peer, c_peer])
+
+    rows = y_ref.shape[2]
+    side = g_ref.shape[-1]
+    pieces = g_ref.shape[1] // side
+    mine = pl.ds(pl.multiple_of(t * rows, 16), rows)
+    order = others + [t]
+    outs = (out_ref, back_ref)
+    sends = []
+
+    def at(ff, tt):
+        return ff * n_tensor + tt
+
+    def go(copy):
+        copy.start()
+        sends.append(copy)
+
+    def arrived(view, sem):
+        remote(view, view, own_sem.at[2], sem, c_peer).wait_recv()
+
+    for k, ff in ((1, f_diag), (0, f_core)):
+        for d, o in enumerate(order):
+            go(remote(g_ref.at[at(ff, o)], c_buf.at[at(k, o)], c_send.at[at(k, d)], c_recv.at[at(k, o)], c_peer))
+    for d, o in enumerate(others):
+        for i in range(2):
+            go(remote(y_ref.at[i, o], outs[i].at[mine], a_send.at[2 * d + i], a_recv.at[2 * t + i], {"tensor": o}))
+    locals_ = [pltpu.make_async_copy(y_ref.at[i, t], outs[i].at[mine], own_sem.at[i]) for i in range(2)]
+    for copy in locals_:
+        copy.start()
+
+    def total(j, *parts):
+        spot = pl.ds(pl.multiple_of(j * side, side), side)
+        return sum(p[i, spot, :].astype(jnp.float32) for p, i in parts)
+
+    for d, o in enumerate(order):
+        arrived(c_buf.at[at(1, o)], c_recv.at[at(1, o)])
+
+        @pl.loop(0, pieces)
+        def _(j):
+            spot = pl.ds(pl.multiple_of(j * side, side), side)
+            y_out[d, spot, :] = total(j, (g_ref, at(f_y, o)), (c_buf, at(1, o))).astype(y_out.dtype)
+
+        go(remote(y_out.at[d], y_buf.at[o], y_send.at[d], y_recv.at[o], y_peer))
+    for d, o in enumerate(others):
+        arrived(c_buf.at[at(0, o)], c_recv.at[at(0, o)])
+        arrived(y_buf.at[o], y_recv.at[o])
+
+        @pl.loop(0, pieces)
+        def _(j):
+            spot = pl.ds(pl.multiple_of(j * side, side), side)
+            parts = (g_ref, at(f, o)), (c_buf, at(0, o)), (y_buf, o)
+            z_out[d, spot, :] = total(j, *parts).astype(z_out.dtype)
+
+        go(remote(z_out.at[d], z_buf.at[t], z_send.at[d], z_recv.at[t], {"tensor": o}))
+    arrived(c_buf.at[at(0, t)], c_recv.at[at(0, t)])
+    arrived(y_buf.at[t], y_recv.at[t])
+    for o in others:
+        arrived(z_buf.at[o], z_recv.at[o])
+    per_share = pieces // 3
+    for m, ref in enumerate((gate_ref, up_ref, down_ref)):
+        for k in range(per_share):
+            parts = [(g_ref, at(f, t)), (c_buf, at(0, t)), (y_buf, t)] + [(z_buf, o) for o in others]
+            ref[0, k] = total(m * per_share + k, *parts).astype(ref.dtype)
+    for o in others:
+        for i in range(2):
+            spot = pl.ds(pl.multiple_of(o * rows, 16), rows)
+            arrived(outs[i].at[spot], a_recv.at[2 * o + i])
+    for copy in locals_:
+        copy.wait()
+    for copy in sends:
+        copy.wait_send()
 
 
 def send_back(n_fsdp, n_tensor, y, grads):
-    own = lax.psum_scatter(grads, ("fsdp", "tensor"), scatter_dimension=0, tiled=True)
-    return lax.all_to_all(y, "tensor", 1, 1, tiled=True), own[0]
+    rows, feats = y.shape[2:]
+    side = grads.shape[-1]
+    unit = grads.shape[1:]
+    per_share = unit[0] // (3 * side)
+    anywhere, vmem = pl.BlockSpec(memory_space=pl.ANY), pl.BlockSpec(memory_space=pltpu.VMEM)
+    sem = pltpu.SemaphoreType.DMA
+    big = jax.ShapeDtypeStruct((n_tensor * rows, feats), y.dtype)
+    small = jax.ShapeDtypeStruct((1, per_share, side, side), grads.dtype)
+
+    def buf(count):
+        return pltpu.VMEM((count,) + unit, grads.dtype)
+
+    return pl.pallas_call(
+        functools.partial(return_kernel, n_tensor),
+        out_shape=(big, big, small, small, small),
+        in_specs=[anywhere, vmem],
+        out_specs=(anywhere, anywhere, vmem, vmem, vmem),
+        scratch_shapes=[
+            buf(2 * n_tensor), buf(n_tensor), buf(n_tensor), buf(n_tensor - 1), buf(n_tensor),
+            sem((2 * n_tensor,)), sem((n_tensor,)), sem((n_tensor - 1,)), sem((2 * n_tensor - 2,)),
+            sem((2 * n_tensor,)), sem((n_tensor,)), sem((n_tensor,)), sem((2 * n_tensor,)), sem((3,)),
+        ],
+        compiler_params=pltpu.CompilerParams(
+            collective_id=1, has_side_effects=True, vmem_limit_bytes=40 * 1024 * 1024
+        ),
+    )(y, grads)
 
 
 def solution(mesh):
@@ -250,7 +457,8 @@
 
     def on_device(*args):
         block_bytes = 3 * args[2].size * args[2].dtype.itemsize * n_fsdp * n_tensor
-        if block_bytes <= 8 * 1024 * 1024 and args[0].shape[0] % (16 * n_tensor) == 0:
+        known = mesh.shape["group"] == 2 and n_fsdp == 4
+        if known and block_bytes <= 8 * 1024 * 1024 and args[0].shape[0] % (16 * n_tensor) == 0:
             return spread_plan(n_fsdp, n_tensor, *args)
         return gathered_plan(*args)
 

time: 178 us -> 119 us (0.67)
  the two profiles are of different devices: /device:TPU:0 before, /device:TPU:12 now
where the time goes in v2:
time: 119 us
  Pallas kernels  107 us (90%)
  local copies, waits for them, and re-layouts  8.72 us (7%)
  other arithmetic  2.86 us (2%)
    pallas_call x1, Pallas kernels, send_back(): pl.pallas_call(functools.partial(return_kernel, n_tensor), out_shape=(big...  51.5 us
    pallas_call x1, Pallas kernels, bring(): pl.pallas_call(functools.partial(bring_kernel, n_tensor), out_shape=(jax....  40.9 us
    pallas_call x1, Pallas kernels, run_blocks(): pl.pallas_call(functools.partial(block_pass, slots, width, shares), out_s...  14.3 us
    unnamed x13, local copies, waits for them, and re-layouts  8.54 us

profile of v2, /device:TPU:12, one launch (start us, length us, event | category | flops | bytes accessed | tf_op | source)
XLA Modules:
  0.0 119.0 jit_solution(8748416091755123396)
XLA Ops:
  0.6 0.7 convert.13
  1.3 0.7 copy.19
  2.0 0.2 reduce_window_sum.14
  2.2 0.1 convert_reduce_fusion
  2.4 0.1 pad_maximum_fusion.1
  2.4 0.1 reshape.28
  2.5 1.7 %pad_maximum_fusion.unit_ref = bf16[1184,128]{1,0:T(8,128)(2,1)} fusion(bf16[32,128]{1,0:T(8,128)(2,1)S(1)} %pad_bitcast_fusion, bf16[384,128]{1,0:T(8,128)(2,1)} %bitcast.16, bf16[384,128]{1,0:T(8,128)(2,1)} %bitcast.17, bf16[384,128]{1,0:T(8,128)(2,1)} %bitcast.18), kind=kLoop, calls=%fused_computation | loop fusion | flops 1212416 | bytes 606208 | tf_op jit(solution)/shard_map/concatenate | solution.py:218
  4.3 40.9 %shard_map.110 = (bf16[16,1184,128]{2,1,0:T(8,128)(2,1)}, bf16[2,4,64,1024]{3,2,1,0:T(8,128)(2,1)}) custom-call(bf16[1184,128]{1,0:T(8,128)(2,1)} %pad_maximum_fusion.unit_ref, bf16[256,1024]{1,0:T(8,128)(2,1)} %tok_ref.1, bf16[256,1024]{1,0:T(8,128)(2,1)} %cot_ref.1), custom_call_target="tpu_custom_call" | custom-call | tf_op jit(solution)/shard_map/pallas_call | solution.py:327
  45.2 0.8 slice_bitcast_fusion
  46.0 0.1 reshape.33.meta_ref
  46.1 0.0 copy-start.1
  46.1 1.2 %copy-done.1 = bf16[2,4,64,1024]{3,2,1,0:T(8,128)(2,1)S(1)} copy-done((bf16[2,4,64,1024]{3,2,1,0:T(8,128)(2,1)S(1)}, bf16[2,4,64,1024]{3,2,1,0:T(8,128)(2,1)}, u32[]{:S(2)}) %copy-start.1) | copy-done | bytes 1048600
  47.3 14.3 %shard_map.111 = (bf16[2,4,64,1024]{3,2,1,0:T(8,128)(2,1)S(1)}, bf16[16,1152,128]{2,1,0:T(8,128)(2,1)}) custom-call(s32[288]{0:T(512)S(1)} %reshape.33.meta_ref, bf16[2,4,64,1024]{3,2,1,0:T(8,128)(2,1)S(1)} %copy-done.1, bf16[16,1184,128]{2,1,0:T(8,128)(2,1)} %get-tuple-element.9.w_ref), custom_call_target="tpu_custom_call" | custom-call | tf_op jit(solution)/shard_map/pallas_call | solution.py:196
  61.6 0.0 copy-start
  61.6 2.3 %copy-done = bf16[16,1152,128]{2,1,0:T(8,128)(2,1)S(1)} copy-done((bf16[16,1152,128]{2,1,0:T(8,128)(2,1)S(1)}, bf16[16,1152,128]{2,1,0:T(8,128)(2,1)}, u32[]{:S(2)}) %copy-start) | copy-done | bytes 4718616
  63.9 51.5 %shard_map.112 = (bf16[256,1024]{1,0:T(8,128)(2,1)S(1)}, bf16[256,1024]{1,0:T(8,128)(2,1)S(1)}, bf16[1,3,128,128]{3,2,1,0:T(8,128)(2,1)S(1)}, bf16[1,3,128,128]{...) custom-call(bf16[2,4,64,1024]{3,2,1,0:T(8,128)(2,1)S(1)} %get-tuple-element.11.y_ref, bf16[16,1152,128]{2,1,0:T(8,128)(2,1)S(1)} %copy-done), custom_call_target="tpu_custom_call" | custom-call | tf_op jit(solution)/shard_map/pallas_call | solution.py:439
  115.5 0.8 copy.26
  116.2 0.8 copy.27
  117.0 0.6 copy.28
  117.7 0.6 copy.29
  118.3 0.6 copy.30
  (5 shorter events, 0.0 us)
Async XLA Ops:
  46.1 1.2 %copy-start.1 = (bf16[2,4,64,1024]{3,2,1,0:T(8,128)(2,1)S(1)}, bf16[2,4,64,1024]{3,2,1,0:T(8,128)(2,1)}, u32[]{:S(2)}) copy-start(bf16[2,4,64,1024]{3,2,1,0:T(8,128)(2,1)} %get-tuple-element.10.acts_ref) | copy-start | bytes 3145732
  61.6 2.3 %copy-start = (bf16[16,1152,128]{2,1,0:T(8,128)(2,1)S(1)}, bf16[16,1152,128]{2,1,0:T(8,128)(2,1)}, u32[]{:S(2)}) copy-start(bf16[16,1152,128]{2,1,0:T(8,128)(2,1)} %get-tuple-element.12.g_ref) | copy-start | bytes 14155780

commit v3 on v2

--- a/solution.py
+++ b/solution.py
@@ -116,7 +116,7 @@
     return (layer_out, input_grad, gate_grad, up_grad, down_grad)
 
 
-def block_pass(slots, width, shares, meta_ref, acts_ref, w_ref, y_ref, g_ref, gate, up, dhid, hid, dgate, dup, acc):
+def block_pass(slots, width, shares, meta_ref, acts_ref, w_ref, y_ref, left_ref, right_ref, gate, up, dhid, hid, dgate, dup, acc):
     n_tensor, tok, feats = acts_ref.shape[1:]
     side = w_ref.shape[-1]
     per_chunk = feats // side
@@ -145,7 +145,7 @@
     def dot(a, b, dims):
         return lax.dot_general(a, b, (dims, ((), ())), preferred_element_type=jnp.float32)
 
-    plain, right_t, left_t = ((1,), (0,)), ((1,), (1,)), ((0,), (0,))
+    plain, right_t = ((1,), (0,)), ((1,), (1,))
     acc[...] = jnp.zeros_like(acc)
 
     @pl.loop(0, n_tensor)
@@ -175,10 +175,11 @@
             picked = [vals[col_of(t, m, s, zero)] for s in range(slots)]
             terms = [dot(picked[s], weight(t, m, s), dims) for s in range(slots)]
             for s in range(slots):
-                unit, at = place(t, m, s)
+                unit, at = s // per_share * n_tensor + t, m * per_share + s % per_share
                 other = act(which, rows[s])
                 pair = (picked[s], other) if m == 2 else (other, picked[s])
-                g_ref[unit, at, :] = dot(*pair, left_t).astype(g_ref.dtype)
+                left_ref[unit, at] = pair[0]
+                right_ref[unit, at] = pair[1]
             for s in range(slots):
                 acc[out, rows[s]] += terms[s]
 
@@ -192,15 +193,13 @@
     n_tensor, tok, feats = acts.shape[1:]
     units, _, side = weights.shape
     vmem = pl.BlockSpec(memory_space=pltpu.VMEM)
+    picked = jax.ShapeDtypeStruct((units, 3 * slots // shares, tok, side), acts.dtype)
     cols = (width + 2, tok, side)
     return pl.pallas_call(
         functools.partial(block_pass, slots, width, shares),
-        out_shape=(
-            jax.ShapeDtypeStruct(acts.shape, acts.dtype),
-            jax.ShapeDtypeStruct((units, 3 * slots // shares * side, side), weights.dtype),
-        ),
+        out_shape=(jax.ShapeDtypeStruct(acts.shape, acts.dtype), picked, picked),
         in_specs=[pl.BlockSpec(memory_space=pltpu.SMEM), vmem, vmem],
-        out_specs=(vmem, vmem),
+        out_specs=(vmem, vmem, vmem),
         scratch_shapes=[pltpu.VMEM(cols, jnp.float32)] * 3
         + [pltpu.VMEM(cols, jnp.bfloat16)] * 3
         + [pltpu.VMEM((2, n_tensor * feats // side, tok, side), jnp.float32)],
@@ -224,8 +223,8 @@
     weights, acts = bring(n_fsdp, n_tensor, unit, tokens, cotangent)
     meta = weights[:n_tensor, -32:, :].astype(jnp.int32).reshape(n_tensor, -1)
     meta = meta[:, : 6 * slots].reshape(-1)
-    y, grads = run_blocks(meta, acts, weights, slots, width, n_fsdp)
-    return send_back(n_fsdp, n_tensor, y, grads)
+    y, lefts, rights = run_blocks(meta, acts, weights, slots, width, n_fsdp)
+    return send_back(n_tensor, y, lefts, rights)
 
 
 def greet(peers):
@@ -251,7 +250,9 @@
     f_y = lax.rem(f + 2, 4)
     f_diag = f_core + f_y - f
     x_peer, y_peer, c_peer = {"group": 1 - group}, {"fsdp": f_y}, {"fsdp": f_core}
-    others = [lax.rem(t + d, n_tensor) for d in range(1, n_tensor)]
+    pair = t + 1 - 2 * lax.rem(t, 2)
+    far = n_tensor - 1 - t
+    others = [pair, far, n_tensor - 1 - pair]
     greet([{"tensor": o} for o in others] + [x_peer, y_peer, c_peer])
 
     half = unit_ref.shape[0] // 2
@@ -274,8 +275,13 @@
     def arrived(view, sem):
         remote(view, view, own_sem.at[0], sem, c_peer).wait_recv()
 
+    def share_acts():
+        for d, o in enumerate(others):
+            for i, ref in enumerate((tok_ref, cot_ref)):
+                go(remote(ref.at[chunk(o)], acts_ref.at[i, t], a_send.at[2 * d + i], a_recv.at[2 * t + i], {"tensor": o}))
+
     me = at(f, t)
-    for d, o in enumerate(others):
+    for d, o in enumerate((far, pair)):
         go(remote(unit_ref.at[mine], w_ref.at[me, mine], z_send.at[d], z_recv.at[t], {"tensor": o}))
     go(remote(unit_ref.at[mine], w_ref.at[me, mine], y_send.at[n_tensor - 1], y_recv.at[t], y_peer))
     go(remote(unit_ref, w_ref.at[me], c_send.at[0], c_recv.at[at(0, t)], c_peer))
@@ -291,11 +297,12 @@
     for d, o in enumerate(others):
         part = w_ref.at[at(f, o), mine]
         arrived(part, z_recv.at[o])
+        if d == 1:
+            go(remote(part, part, z_send.at[2], z_recv.at[o], {"tensor": pair}))
         go(remote(part, part, y_send.at[d], y_recv.at[o], y_peer))
         go(remote(part, part, x_send.at[1 + d], x_recv.at[at(0, o)], x_peer))
-    for d, o in enumerate(others):
-        for i, ref in enumerate((tok_ref, cot_ref)):
-            go(remote(ref.at[chunk(o)], acts_ref.at[i, t], a_send.at[2 * d + i], a_recv.at[2 * t + i], {"tensor": o}))
+        if d == 1:
+            share_acts()
     for d, o in enumerate(others):
         part = w_ref.at[at(f_y, o), mine]
         arrived(part, y_recv.at[o])
@@ -341,22 +348,23 @@
 
 
 def return_kernel(
-    n_tensor, y_ref, g_ref, out_ref, back_ref, gate_ref, up_ref, down_ref,
-    c_buf, y_out, y_buf, z_out, z_buf, c_send, y_send, z_send, a_send, c_recv, y_recv, z_recv, a_recv, own_sem,
+    n_tensor, y_ref, left_ref, right_ref, out_ref, back_ref, gate_ref, up_ref, down_ref,
+    c_out, c_buf, y_out, y_buf, z_out, z_buf, c_send, y_send, z_send, a_send, c_recv, y_recv, z_recv, a_recv, own_sem,
 ):
     f, t = lax.axis_index("fsdp"), lax.axis_index("tensor")
     f_core = f + 1 - 2 * lax.rem(f, 2)
     f_y = lax.rem(f + 2, 4)
     f_diag = f_core + f_y - f
-    y_peer, c_peer = {"fsdp": f_y}, {"fsdp": f_core}
-    others = [lax.rem(t + d, n_tensor) for d in range(1, n_tensor)]
+    pair = t + 1 - 2 * lax.rem(t, 2)
+    far = n_tensor - 1 - t
+    y_peer, c_peer, pair_peer, far_peer = {"fsdp": f_y}, {"fsdp": f_core}, {"tensor": pair}, {"tensor": far}
+    others = [n_tensor - 1 - pair, far, pair]
+    order = others + [t]
     greet([{"tensor": o} for o in others] + [y_peer, c_peer])
 
     rows = y_ref.shape[2]
-    side = g_ref.shape[-1]
-    pieces = g_ref.shape[1] // side
+    pieces = left_ref.shape[1]
     mine = pl.ds(pl.multiple_of(t * rows, 16), rows)
-    order = others + [t]
     outs = (out_ref, back_ref)
     sends = []
 
@@ -370,9 +378,6 @@
     def arrived(view, sem):
         remote(view, view, own_sem.at[2], sem, c_peer).wait_recv()
 
-    for k, ff in ((1, f_diag), (0, f_core)):
-        for d, o in enumerate(order):
-            go(remote(g_ref.at[at(ff, o)], c_buf.at[at(k, o)], c_send.at[at(k, d)], c_recv.at[at(k, o)], c_peer))
     for d, o in enumerate(others):
         for i in range(2):
             go(remote(y_ref.at[i, o], outs[i].at[mine], a_send.at[2 * d + i], a_recv.at[2 * t + i], {"tensor": o}))
@@ -380,39 +385,46 @@
     for copy in locals_:
         copy.start()
 
-    def total(j, *parts):
-        spot = pl.ds(pl.multiple_of(j * side, side), side)
-        return sum(p[i, spot, :].astype(jnp.float32) for p, i in parts)
-
-    for d, o in enumerate(order):
-        arrived(c_buf.at[at(1, o)], c_recv.at[at(1, o)])
-
+    def total(unit, j, *parts):
+        own = lax.dot_general(
+            left_ref[unit, j], right_ref[unit, j], (((0,), (0,)), ((), ())), preferred_element_type=jnp.float32
+        )
+        return sum([ref[i, j].astype(jnp.float32) for ref, i in parts], own)
+
+    def fill(dst, slot, unit, *parts):
         @pl.loop(0, pieces)
         def _(j):
-            spot = pl.ds(pl.multiple_of(j * side, side), side)
-            y_out[d, spot, :] = total(j, (g_ref, at(f_y, o)), (c_buf, at(1, o))).astype(y_out.dtype)
-
-        go(remote(y_out.at[d], y_buf.at[o], y_send.at[d], y_recv.at[o], y_peer))
-    for d, o in enumerate(others):
-        arrived(c_buf.at[at(0, o)], c_recv.at[at(0, o)])
-        arrived(y_buf.at[o], y_recv.at[o])
-
-        @pl.loop(0, pieces)
-        def _(j):
-            spot = pl.ds(pl.multiple_of(j * side, side), side)
-            parts = (g_ref, at(f, o)), (c_buf, at(0, o)), (y_buf, o)
-            z_out[d, spot, :] = total(j, *parts).astype(z_out.dtype)
-
-        go(remote(z_out.at[d], z_buf.at[t], z_send.at[d], z_recv.at[t], {"tensor": o}))
-    arrived(c_buf.at[at(0, t)], c_recv.at[at(0, t)])
-    arrived(y_buf.at[t], y_recv.at[t])
-    for o in others:
-        arrived(z_buf.at[o], z_recv.at[o])
+            dst[slot, j] = total(unit, j, *parts).astype(dst.dtype)
+
+    for k, ff in ((1, f_diag), (0, f_core)):
+        for d, o in enumerate(order):
+            fill(c_out, at(k, d), at(ff, o))
+            go(remote(c_out.at[at(k, d)], c_buf.at[at(k, d)], c_send.at[at(k, d)], c_recv.at[at(k, d)], c_peer))
+        if k == 1:
+            for d, o in enumerate(order):
+                arrived(c_buf.at[at(1, d)], c_recv.at[at(1, d)])
+                fill(y_out, d, at(f_y, o), (c_buf, at(1, d)))
+                go(remote(y_out.at[d], y_buf.at[d], y_send.at[d], y_recv.at[d], y_peer))
+
+    def near(d):
+        arrived(c_buf.at[at(0, d)], c_recv.at[at(0, d)])
+        arrived(y_buf.at[d], y_recv.at[d])
+        return (c_buf, at(0, d)), (y_buf, d)
+
+    for slot, (d, peer) in enumerate(((0, pair_peer), (2, pair_peer), (1, far_peer))):
+        parts = near(d)
+        if slot == 2:
+            arrived(z_buf.at[0], z_recv.at[0])
+            parts = parts + ((z_buf, 0),)
+        fill(z_out, slot, at(f, order[d]), *parts)
+        go(remote(z_out.at[slot], z_buf.at[slot], z_send.at[slot], z_recv.at[slot], peer))
+    parts = near(3) + ((z_buf, 1), (z_buf, 2))
+    arrived(z_buf.at[1], z_recv.at[1])
+    arrived(z_buf.at[2], z_recv.at[2])
     per_share = pieces // 3
     for m, ref in enumerate((gate_ref, up_ref, down_ref)):
         for k in range(per_share):
-            parts = [(g_ref, at(f, t)), (c_buf, at(0, t)), (y_buf, t)] + [(z_buf, o) for o in others]
-            ref[0, k] = total(m * per_share + k, *parts).astype(ref.dtype)
+            ref[0, k] = total(at(f, t), m * per_share + k, *parts).astype(ref.dtype)
     for o in others:
         for i in range(2):
             spot = pl.ds(pl.multiple_of(o * rows, 16), rows)
@@ -423,33 +435,31 @@
         copy.wait_send()
 
 
-def send_back(n_fsdp, n_tensor, y, grads):
+def send_back(n_tensor, y, lefts, rights):
     rows, feats = y.shape[2:]
-    side = grads.shape[-1]
-    unit = grads.shape[1:]
-    per_share = unit[0] // (3 * side)
+    pieces, _, side = lefts.shape[1:]
     anywhere, vmem = pl.BlockSpec(memory_space=pl.ANY), pl.BlockSpec(memory_space=pltpu.VMEM)
     sem = pltpu.SemaphoreType.DMA
     big = jax.ShapeDtypeStruct((n_tensor * rows, feats), y.dtype)
-    small = jax.ShapeDtypeStruct((1, per_share, side, side), grads.dtype)
+    small = jax.ShapeDtypeStruct((1, pieces // 3, side, side), y.dtype)
 
     def buf(count):
-        return pltpu.VMEM((count,) + unit, grads.dtype)
+        return pltpu.VMEM((count, pieces, side, side), y.dtype)
 
     return pl.pallas_call(
         functools.partial(return_kernel, n_tensor),
         out_shape=(big, big, small, small, small),
-        in_specs=[anywhere, vmem],
+        in_specs=[anywhere, vmem, vmem],
         out_specs=(anywhere, anywhere, vmem, vmem, vmem),
         scratch_shapes=[
-            buf(2 * n_tensor), buf(n_tensor), buf(n_tensor), buf(n_tensor - 1), buf(n_tensor),
+            buf(2 * n_tensor), buf(2 * n_tensor), buf(n_tensor), buf(n_tensor), buf(n_tensor - 1), buf(n_tensor - 1),
             sem((2 * n_tensor,)), sem((n_tensor,)), sem((n_tensor - 1,)), sem((2 * n_tensor - 2,)),
-            sem((2 * n_tensor,)), sem((n_tensor,)), sem((n_tensor,)), sem((2 * n_tensor,)), sem((3,)),
+            sem((2 * n_tensor,)), sem((n_tensor,)), sem((n_tensor - 1,)), sem((2 * n_tensor,)), sem((3,)),
         ],
         compiler_params=pltpu.CompilerParams(
             collective_id=1, has_side_effects=True, vmem_limit_bytes=40 * 1024 * 1024
         ),
-    )(y, grads)
+    )(y, lefts, rights)
 
 
 def solution(mesh):
@@ -457,7 +467,7 @@
 
     def on_device(*args):
         block_bytes = 3 * args[2].size * args[2].dtype.itemsize * n_fsdp * n_tensor
-        known = mesh.shape["group"] == 2 and n_fsdp == 4
+        known = mesh.shape["group"] == 2 and n_fsdp == 4 and n_tensor == 4
         if known and block_bytes <= 8 * 1024 * 1024 and args[0].shape[0] % (16 * n_tensor) == 0:
             return spread_plan(n_fsdp, n_tensor, *args)
         return gathered_plan(*args)

time: 119 us -> 110 us (0.924)
  the two profiles are of different devices: /device:TPU:12 before, /device:TPU:0 now
where the time goes in v3:
time: 110 us; the launch traced here: 109 us
  Pallas kernels  97.7 us (89%)
  local copies, waits for them, and re-layouts  8.05 us (7%)
  other arithmetic  2.86 us (3%)
    pallas_call x1, Pallas kernels, send_back(): pl.pallas_call(functools.partial(return_kernel, n_tensor), out_shape=(big...  47.8 us
    pallas_call x1, Pallas kernels, bring(): pl.pallas_call(functools.partial(bring_kernel, n_tensor), out_shape=(jax....  37.7 us
    pallas_call x1, Pallas kernels, run_blocks(): pl.pallas_call(functools.partial(block_pass, slots, width, shares), out_s...  12.2 us
    unnamed x13, local copies, waits for them, and re-layouts  7.87 us

profile of v3, /device:TPU:0, one launch (start us, length us, event | category | flops | bytes accessed | tf_op | source)
XLA Modules:
  0.0 109.3 jit_solution(6395195516726135684)
XLA Ops:
  0.6 0.7 convert.13
  1.3 0.7 copy.19
  2.0 0.2 reduce_window_sum.14
  2.2 0.1 convert_reduce_fusion
  2.4 0.1 pad_maximum_fusion.1
  2.4 0.1 reshape.28
  2.5 1.7 %pad_maximum_fusion.unit_ref = bf16[1184,128]{1,0:T(8,128)(2,1)} fusion(bf16[32,128]{1,0:T(8,128)(2,1)S(1)} %pad_bitcast_fusion, bf16[384,128]{1,0:T(8,128)(2,1)} %bitcast.16, bf16[384,128]{1,0:T(8,128)(2,1)} %bitcast.17, bf16[384,128]{1,0:T(8,128)(2,1)} %bitcast.18), kind=kLoop, calls=%fused_computation | loop fusion | flops 1212416 | bytes 606208 | tf_op jit(solution)/shard_map/concatenate | solution.py:217
  4.3 37.7 %shard_map.110 = (bf16[16,1184,128]{2,1,0:T(8,128)(2,1)}, bf16[2,4,64,1024]{3,2,1,0:T(8,128)(2,1)}) custom-call(bf16[1184,128]{1,0:T(8,128)(2,1)} %pad_maximum_fusion.unit_ref, bf16[256,1024]{1,0:T(8,128)(2,1)} %tok_ref.1, bf16[256,1024]{1,0:T(8,128)(2,1)} %cot_ref.1), custom_call_target="tpu_custom_call" | custom-call | tf_op jit(solution)/shard_map/pallas_call | solution.py:334
  41.9 0.8 slice_bitcast_fusion
  42.7 0.1 reshape.33.meta_ref
  42.8 0.0 copy-start.1
  42.8 1.2 %copy-done.1 = bf16[2,4,64,1024]{3,2,1,0:T(8,128)(2,1)S(1)} copy-done((bf16[2,4,64,1024]{3,2,1,0:T(8,128)(2,1)S(1)}, bf16[2,4,64,1024]{3,2,1,0:T(8,128)(2,1)}, u32[]{:S(2)}) %copy-start.1) | copy-done | bytes 1048600
  44.0 12.2 %shard_map.111 = (bf16[2,4,64,1024]{3,2,1,0:T(8,128)(2,1)S(1)}, bf16[16,9,64,128]{3,2,1,0:T(8,128)(2,1)S(1)}, bf16[16,9,64,128]{3,2,1,0:T(8,128)(2,1)}) custom-call(s32[288]{0:T(512)S(1)} %reshape.33.meta_ref, bf16[2,4,64,1024]{3,2,1,0:T(8,128)(2,1)S(1)} %copy-done.1, bf16[16,1184,128]{2,1,0:T(8,128)(2,1)} %get-tuple-element.10.w_ref), custom_call_target="tpu_custom_call" | custom-call | tf_op jit(solution)/shard_map/pallas_call | solution.py:198
  56.3 0.0 copy-start
  56.3 1.7 %copy-done = bf16[16,9,64,128]{3,2,1,0:T(8,128)(2,1)S(1)} copy-done((bf16[16,9,64,128]{3,2,1,0:T(8,128)(2,1)S(1)}, bf16[16,9,64,128]{3,2,1,0:T(8,128)(2,1)}, u32[]{:S(2)}) %copy-start) | copy-done | bytes 2359320
  57.9 47.8 %shard_map.112 = (bf16[256,1024]{1,0:T(8,128)(2,1)S(1)}, bf16[256,1024]{1,0:T(8,128)(2,1)S(1)}, bf16[1,3,128,128]{3,2,1,0:T(8,128)(2,1)S(1)}, bf16[1,3,128,128]{...) custom-call(bf16[2,4,64,1024]{3,2,1,0:T(8,128)(2,1)S(1)} %get-tuple-element.12.y_ref, ...), custom_call_target="tpu_custom_call" | custom-call | tf_op jit(solution)/shard_map/pallas_call | solution.py:449
  105.8 0.8 copy.26
  106.6 0.8 copy.27
  107.4 0.6 copy.28
  108.0 0.6 copy.29
  108.6 0.6 copy.30
  (5 shorter events, 0.0 us)
Async XLA Ops:
  42.8 1.2 %copy-start.1 = (bf16[2,4,64,1024]{3,2,1,0:T(8,128)(2,1)S(1)}, bf16[2,4,64,1024]{3,2,1,0:T(8,128)(2,1)}, u32[]{:S(2)}) copy-start(bf16[2,4,64,1024]{3,2,1,0:T(8,128)(2,1)} %get-tuple-element.11.acts_ref) | copy-start | bytes 3145732
  56.3 1.7 %copy-start = (bf16[16,9,64,128]{3,2,1,0:T(8,128)(2,1)S(1)}, bf16[16,9,64,128]{3,2,1,0:T(8,128)(2,1)}, u32[]{:S(2)}) copy-start(bf16[16,9,64,128]{3,2,1,0:T(8,128)(2,1)} %get-tuple-element.14.right_ref) | copy-start | bytes 7077892

commit v4 on v3

--- a/solution.py
+++ b/solution.py
@@ -203,7 +203,7 @@
         scratch_shapes=[pltpu.VMEM(cols, jnp.float32)] * 3
         + [pltpu.VMEM(cols, jnp.bfloat16)] * 3
         + [pltpu.VMEM((2, n_tensor * feats // side, tok, side), jnp.float32)],
-        compiler_params=pltpu.CompilerParams(vmem_limit_bytes=48 * 1024 * 1024),
+        compiler_params=pltpu.CompilerParams(vmem_limit_bytes=24 * 1024 * 1024),
     )(meta, acts, weights)
 
 
@@ -275,15 +275,15 @@
     def arrived(view, sem):
         remote(view, view, own_sem.at[0], sem, c_peer).wait_recv()
 
-    def share_acts():
+    def share_acts(i):
+        ref = (tok_ref, cot_ref)[i]
         for d, o in enumerate(others):
-            for i, ref in enumerate((tok_ref, cot_ref)):
-                go(remote(ref.at[chunk(o)], acts_ref.at[i, t], a_send.at[2 * d + i], a_recv.at[2 * t + i], {"tensor": o}))
+            go(remote(ref.at[chunk(o)], acts_ref.at[i, t], a_send.at[2 * d + i], a_recv.at[2 * t + i], {"tensor": o}))
 
     me = at(f, t)
     for d, o in enumerate((far, pair)):
         go(remote(unit_ref.at[mine], w_ref.at[me, mine], z_send.at[d], z_recv.at[t], {"tensor": o}))
-    go(remote(unit_ref.at[mine], w_ref.at[me, mine], y_send.at[n_tensor - 1], y_recv.at[t], y_peer))
+    go(remote(unit_ref, w_ref.at[me], y_send.at[n_tensor - 1], y_recv.at[t], y_peer))
     go(remote(unit_ref, w_ref.at[me], c_send.at[0], c_recv.at[at(0, t)], c_peer))
     locals_ = [pltpu.make_async_copy(unit_ref, w_ref.at[me], own_sem.at[1])]
     for i, ref in enumerate((tok_ref, cot_ref)):
@@ -291,24 +291,22 @@
     for copy in locals_:
         copy.start()
 
-    arrived(w_ref.at[at(f_y, t), mine], y_recv.at[t])
-    part = w_ref.at[at(f_y, t), mine]
-    go(remote(part, part, x_send.at[0], x_recv.at[at(1, t)], x_peer))
+    share_acts(0)
     for d, o in enumerate(others):
         part = w_ref.at[at(f, o), mine]
         arrived(part, z_recv.at[o])
         if d == 1:
             go(remote(part, part, z_send.at[2], z_recv.at[o], {"tensor": pair}))
         go(remote(part, part, y_send.at[d], y_recv.at[o], y_peer))
-        go(remote(part, part, x_send.at[1 + d], x_recv.at[at(0, o)], x_peer))
+        go(remote(part, part, x_send.at[d], x_recv.at[at(0, o)], x_peer))
         if d == 1:
-            share_acts()
+            share_acts(1)
     for d, o in enumerate(others):
         part = w_ref.at[at(f_y, o), mine]
         arrived(part, y_recv.at[o])
-        go(remote(part, part, x_send.at[n_tensor + d], x_recv.at[at(1, o)], x_peer))
+        go(remote(part, part, x_send.at[n_tensor - 1 + d], x_recv.at[at(1, o)], x_peer))
     part = w_ref.at[at(f_y, t)]
-    arrived(w_ref.at[at(f_y, t), theirs], x_recv.at[at(1, t)])
+    arrived(part, y_recv.at[t])
     go(remote(part, part, c_send.at[1], c_recv.at[at(1, t)], c_peer))
     for k, ff in enumerate((f, f_y)):
         for d, o in enumerate(others):
@@ -340,10 +338,12 @@
         in_specs=[anywhere] * 3,
         out_specs=(anywhere,) * 2,
         scratch_shapes=[
-            sem((n_tensor - 1,)), sem((n_tensor,)), sem((2 * n_tensor - 1,)), sem((2 * n_tensor,)), sem((2 * n_tensor - 2,)),
+            sem((n_tensor - 1,)), sem((n_tensor,)), sem((2 * n_tensor - 2,)), sem((2 * n_tensor,)), sem((2 * n_tensor - 2,)),
             sem((n_tensor,)), sem((n_tensor,)), sem((2 * n_tensor,)), sem((2 * n_tensor,)), sem((2 * n_tensor,)), sem((4,)),
         ],
-        compiler_params=pltpu.CompilerParams(collective_id=0, has_side_effects=True),
+        compiler_params=pltpu.CompilerParams(
+            collective_id=0, has_side_effects=True, vmem_limit_bytes=2 * 1024 * 1024
+        ),
     )(unit, tokens, cotangent)
 
 
@@ -378,9 +378,11 @@
     def arrived(view, sem):
         remote(view, view, own_sem.at[2], sem, c_peer).wait_recv()
 
-    for d, o in enumerate(others):
-        for i in range(2):
+    def share_out(i):
+        for d, o in enumerate(others):
             go(remote(y_ref.at[i, o], outs[i].at[mine], a_send.at[2 * d + i], a_recv.at[2 * t + i], {"tensor": o}))
+
+    share_out(0)
     locals_ = [pltpu.make_async_copy(y_ref.at[i, t], outs[i].at[mine], own_sem.at[i]) for i in range(2)]
     for copy in locals_:
         copy.start()
@@ -418,6 +420,8 @@
             parts = parts + ((z_buf, 0),)
         fill(z_out, slot, at(f, order[d]), *parts)
         go(remote(z_out.at[slot], z_buf.at[slot], z_send.at[slot], z_recv.at[slot], peer))
+        if slot == 0:
+            share_out(1)
     parts = near(3) + ((z_buf, 1), (z_buf, 2))
     arrived(z_buf.at[1], z_recv.at[1])
     arrived(z_buf.at[2], z_recv.at[2])
@@ -457,7 +461,7 @@
             sem((2 * n_tensor,)), sem((n_tensor,)), sem((n_tensor - 1,)), sem((2 * n_tensor,)), sem((3,)),
         ],
         compiler_params=pltpu.CompilerParams(
-            collective_id=1, has_side_effects=True, vmem_limit_bytes=40 * 1024 * 1024
+            collective_id=1, has_side_effects=True, vmem_limit_bytes=24 * 1024 * 1024
         ),
     )(y, lefts, rights)
 

time: 110 us -> 119 us (1.082)
  Pallas kernels: 97.7 us -> 105 us
  local copies, waits for them, and re-layouts: 8.05 us -> 11 us
    pallas_call x1, Pallas kernels: 47.8 us -> 56.6 us  [send_back(): pl.pallas_call(functools.partial(return_kernel, n_tensor), out_shape=(big...]
    pallas_call x1, Pallas kernels: 12.2 us -> 9.14 us  [run_blocks(): pl.pallas_call(functools.partial(block_pass, slots, width, shares), out_s...]
    unnamed x13 -> x17, local copies, waits for them, and re-layouts: 7.87 us -> 10.8 us
    pallas_call x1, Pallas kernels: 37.7 us -> 39 us  [bring(): pl.pallas_call(functools.partial(bring_kernel, n_tensor), out_shape=(jax....]
where the time goes in v4:
time: 119 us
  Pallas kernels  105 us (88%)
  local copies, waits for them, and re-layouts  11 us (9%)
  other arithmetic  2.14 us (2%)
    pallas_call x1, Pallas kernels, send_back(): pl.pallas_call(functools.partial(return_kernel, n_tensor), out_shape=(big...  56.6 us
    pallas_call x1, Pallas kernels, bring(): pl.pallas_call(functools.partial(bring_kernel, n_tensor), out_shape=(jax....  39 us
    unnamed x17, local copies, waits for them, and re-layouts  10.8 us
    pallas_call x1, Pallas kernels, run_blocks(): pl.pallas_call(functools.partial(block_pass, slots, width, shares), out_s...  9.14 us

profile of v4, /device:TPU:0, one launch (start us, length us, event | category | flops | bytes accessed | tf_op | source)
XLA Modules:
  0.0 118.6 jit_solution(14300317192613871738)
XLA Ops:
  0.6 0.7 convert.13
  1.3 0.7 copy.19
  2.0 0.2 reduce_window_sum.14
  2.2 0.1 convert_reduce_fusion
  2.4 0.1 pad_maximum_fusion.1
  2.4 0.1 reshape.28
  2.5 1.0 pad_maximum_fusion.unit_ref
  3.6 0.0 copy-start.2
  3.6 1.0 copy-done.2
  4.6 0.0 copy-start.3
  4.6 1.0 copy-done.3
  5.6 39.0 %shard_map.110 = (bf16[16,1184,128]{2,1,0:T(8,128)(2,1)S(1)}, bf16[2,4,64,1024]{3,2,1,0:T(8,128)(2,1)S(1)}) custom-call(bf16[1184,128]{1,0:T(8,128)(2,1)S(1)} %pad_maximum_fusion.unit_ref, bf16[256,1024]{1,0:T(8,128)(2,1)S(1)} %copy-done.2, bf16[256,1024]{1,0:T(8,128)(2,1)S(1)} %copy-done.3), custom_call_target="tpu_custom_call" | custom-call | tf_op jit(solution)/shard_map/pallas_call | solution.py:332
  44.7 0.0 copy-start
  44.7 2.2 %copy-done = bf16[16,1184,128]{2,1,0:T(8,128)(2,1)} copy-done((bf16[16,1184,128]{2,1,0:T(8,128)(2,1)}, bf16[16,1184,128]{2,1,0:T(8,128)(2,1)S(1)}, u32[]{:S(2)}) %copy-start) | copy-done | bytes 4849688
  46.9 0.1 reshape.33.meta_ref
  47.0 0.0 copy-start.1
  47.0 2.4 %copy-done.1 = bf16[16,1184,128]{2,1,0:T(8,128)(2,1)S(1)} copy-done((bf16[16,1184,128]{2,1,0:T(8,128)(2,1)S(1)}, bf16[16,1184,128]{2,1,0:T(8,128)(2,1)}, u32[]{:S(2)}) %copy-start.1) | copy-done | bytes 4849688
  49.4 9.1 %shard_map.111 = (bf16[2,4,64,1024]{3,2,1,0:T(8,128)(2,1)S(1)}, bf16[16,9,64,128]{3,2,1,0:T(8,128)(2,1)S(1)}, bf16[16,9,64,128]{3,2,1,0:T(8,128)(2,1)S(1)}) custom-call(s32[288]{0:T(512)S(1)} %reshape.33.meta_ref, bf16[2,4,64,1024]{3,2,1,0:T(8,128)(2,1)S(1)} %get-tuple-element.11.acts_ref, bf16[16,1184,128]{2,1,0:T(8,128)(2,1)S(1)} %copy-done.1), custom_call_target="tpu_custom_call" | custom-call | tf_op jit(solution)/shard_map/pallas_call | solution.py:198
  58.5 56.6 %shard_map.112 = (bf16[256,1024]{1,0:T(8,128)(2,1)S(1)}, bf16[256,1024]{1,0:T(8,128)(2,1)S(1)}, bf16[1,3,128,128]{3,2,1,0:T(8,128)(2,1)S(1)}, bf16[1,3,128,128]{...) custom-call(bf16[2,4,64,1024]{3,2,1,0:T(8,128)(2,1)S(1)} %get-tuple-element.12.y_ref, ...), custom_call_target="tpu_custom_call" | custom-call | tf_op jit(solution)/shard_map/pallas_call | solution.py:453
  115.1 0.8 copy.26
  115.9 0.8 copy.27
  116.7 0.6 copy.28
  117.4 0.6 copy.29
  118.0 0.6 copy.30
  (6 shorter events, 0.0 us)
Async XLA Ops:
  3.6 1.0 copy-start.2
  4.6 1.0 copy-start.3
  44.7 2.2 %copy-start = (bf16[16,1184,128]{2,1,0:T(8,128)(2,1)}, bf16[16,1184,128]{2,1,0:T(8,128)(2,1)S(1)}, u32[]{:S(2)}) copy-start(bf16[16,1184,128]{2,1,0:T(8,128)(2,1)S(1)} %get-tuple-element.10.w_ref) | copy-start | bytes 14548996
  47.0 2.4 %copy-start.1 = (bf16[16,1184,128]{2,1,0:T(8,128)(2,1)S(1)}, bf16[16,1184,128]{2,1,0:T(8,128)(2,1)}, u32[]{:S(2)}) copy-start(bf16[16,1184,128]{2,1,0:T(8,128)(2,1)} %copy-done) | copy-start | bytes 14548996

commit v5 on v4

--- a/solution.py
+++ b/solution.py
@@ -116,18 +116,29 @@
     return (layer_out, input_grad, gate_grad, up_grad, down_grad)
 
 
-def block_pass(slots, width, shares, meta_ref, acts_ref, w_ref, y_ref, left_ref, right_ref, gate, up, dhid, hid, dgate, dup, acc):
-    n_tensor, tok, feats = acts_ref.shape[1:]
+def block_pass(slots, width, shares, meta_ref, acts_hbm, w_hbm, y_ref, left_ref, right_ref, gate, up, dhid, hid, dgate, dup, acc, acts_ref, w_ref, acts_sem, w_sem):
+    n_tensor, tok, feats = acts_hbm.shape[1:]
+
+    def load(t, buf):
+        return [
+            pltpu.make_async_copy(w_hbm.at[share * n_tensor + t], w_ref.at[buf * shares + share], w_sem.at[buf, share])
+            for share in range(shares)
+        ]
+
+    acts_copy = pltpu.make_async_copy(acts_hbm, acts_ref, acts_sem)
+    acts_copy.start()
+    for copy in load(0, 0):
+        copy.start()
     side = w_ref.shape[-1]
     per_chunk = feats // side
     per_share = slots // shares
     trash, zero = width, width + 1
 
     def row_of(t, m, s):
-        return meta_ref[t * 6 * slots + m * 2 * slots + s]
+        return meta_ref[t, m, s]
 
     def col_of(t, m, s, dead):
-        col = meta_ref[t * 6 * slots + m * 2 * slots + slots + s]
+        col = meta_ref[t, 3 + m, s]
         return jnp.where(col < width, col, dead)
 
     def act(which, row):
@@ -136,7 +147,7 @@
 
     def place(t, m, s):
         share, k = divmod(s, per_share)
-        return share * n_tensor + t, pl.ds((m * per_share + k) * side, side)
+        return lax.rem(t, 2) * shares + share, pl.ds((m * per_share + k) * side, side)
 
     def weight(t, m, s):
         unit, rows = place(t, m, s)
@@ -147,12 +158,21 @@
 
     plain, right_t = ((1,), (0,)), ((1,), (1,))
     acc[...] = jnp.zeros_like(acc)
+    acts_copy.wait()
 
     @pl.loop(0, n_tensor)
     def _(t):
         gate[...] = jnp.zeros_like(gate)
         up[...] = jnp.zeros_like(up)
         dhid[...] = jnp.zeros_like(dhid)
+        for copy in load(t, lax.rem(t, 2)):
+            copy.wait()
+
+        @pl.when(t + 1 < n_tensor)
+        def _():
+            for copy in load(t + 1, lax.rem(t + 1, 2)):
+                copy.start()
+
         for m, which, dims, into in ((0, 0, plain, gate), (1, 0, plain, up), (2, 1, right_t, dhid)):
             terms = [dot(act(which, row_of(t, m, s)), weight(t, m, s), dims) for s in range(slots)]
             for s in range(slots):
@@ -198,31 +218,25 @@
     return pl.pallas_call(
         functools.partial(block_pass, slots, width, shares),
         out_shape=(jax.ShapeDtypeStruct(acts.shape, acts.dtype), picked, picked),
-        in_specs=[pl.BlockSpec(memory_space=pltpu.SMEM), vmem, vmem],
+        in_specs=[pl.BlockSpec(memory_space=pltpu.SMEM)] + [pl.BlockSpec(memory_space=pl.ANY)] * 2,
         out_specs=(vmem, vmem, vmem),
         scratch_shapes=[pltpu.VMEM(cols, jnp.float32)] * 3
         + [pltpu.VMEM(cols, jnp.bfloat16)] * 3
-        + [pltpu.VMEM((2, n_tensor * feats // side, tok, side), jnp.float32)],
+        + [
+            pltpu.VMEM((2, n_tensor * feats // side, tok, side), jnp.float32),
+            pltpu.VMEM(acts.shape, acts.dtype),
+            pltpu.VMEM((2 * shares,) + weights.shape[1:], weights.dtype),
+            pltpu.SemaphoreType.DMA,
+            pltpu.SemaphoreType.DMA((2, shares)),
+        ],
         compiler_params=pltpu.CompilerParams(vmem_limit_bytes=24 * 1024 * 1024),
     )(meta, acts, weights)
 
 
-def pack_unit(gate_blocks, up_blocks, down_blocks, block_rows, col_counts):
-    slots = block_rows.shape[-1]
-    side = gate_blocks.shape[-1]
-    cols = jax.vmap(lambda c: slot_columns(c, slots))(col_counts[:, 0, :])
-    table = jnp.concatenate([block_rows[:, 0, :], cols], axis=1).reshape(-1)
-    table = jnp.pad(table, (0, 32 * side - table.shape[0])).reshape(32, side)
-    blocks = [b[0].reshape(-1, side) for b in (gate_blocks, up_blocks, down_blocks)]
-    return jnp.concatenate(blocks + [table.astype(jnp.bfloat16)], axis=0)
-
-
 def spread_plan(n_fsdp, n_tensor, tokens, cotangent, gate_blocks, up_blocks, down_blocks, block_rows, col_counts):
     slots, width = block_rows.shape[-1], col_counts.shape[-1]
-    unit = pack_unit(gate_blocks, up_blocks, down_blocks, block_rows, col_counts)
-    weights, acts = bring(n_fsdp, n_tensor, unit, tokens, cotangent)
-    meta = weights[:n_tensor, -32:, :].astype(jnp.int32).reshape(n_tensor, -1)
-    meta = meta[:, : 6 * slots].reshape(-1)
+    blocks = (gate_blocks[0], up_blocks[0], down_blocks[0])
+    weights, acts, meta = bring(n_fsdp, n_tensor, blocks, tokens, cotangent, block_rows, col_counts)
     y, lefts, rights = run_blocks(meta, acts, weights, slots, width, n_fsdp)
     return send_back(n_tensor, y, lefts, rights)
 
@@ -242,8 +256,8 @@
 
 
 def bring_kernel(
-    n_tensor, unit_ref, tok_ref, cot_ref, w_ref, acts_ref,
-    z_send, y_send, x_send, c_send, a_send, z_recv, y_recv, x_recv, c_recv, a_recv, own_sem,
+    n_tensor, gate_ref, up_ref, down_ref, tok_ref, cot_ref, rows_ref, counts_ref, w_ref, acts_ref, tables_ref, table,
+    z_send, y_send, x_send, c_send, a_send, z_recv, y_recv, x_recv, c_recv, a_recv, t_send, t_recv, own_sem,
 ):
     group, f, t = (lax.axis_index(a) for a in ("group", "fsdp", "tensor"))
     f_core = f + 1 - 2 * lax.rem(f, 2)
@@ -253,9 +267,20 @@
     pair = t + 1 - 2 * lax.rem(t, 2)
     far = n_tensor - 1 - t
     others = [pair, far, n_tensor - 1 - pair]
+    me = f * n_tensor + t
+    part_rows = gate_ref.shape[0]
+    blocks = [
+        pltpu.make_async_copy(ref, w_ref.at[me, pl.ds(m * part_rows, part_rows)], own_sem.at[4 + m])
+        for m, ref in enumerate((gate_ref, up_ref, down_ref))
+    ]
+    for copy in blocks:
+        copy.start()
     greet([{"tensor": o} for o in others] + [x_peer, y_peer, c_peer])
-
-    half = unit_ref.shape[0] // 2
+    for copy in blocks:
+        copy.wait()
+
+    unit_ref = w_ref.at[me]
+    half = w_ref.shape[1] // 2
     mine = pl.ds(pl.multiple_of(group * half, 16), half)
     theirs = pl.ds(pl.multiple_of((1 - group) * half, 16), half)
     rows = tok_ref.shape[0] // n_tensor
@@ -280,18 +305,27 @@
         for d, o in enumerate(others):
             go(remote(ref.at[chunk(o)], acts_ref.at[i, t], a_send.at[2 * d + i], a_recv.at[2 * t + i], {"tensor": o}))
 
-    me = at(f, t)
     for d, o in enumerate((far, pair)):
-        go(remote(unit_ref.at[mine], w_ref.at[me, mine], z_send.at[d], z_recv.at[t], {"tensor": o}))
+        go(remote(w_ref.at[me, mine], w_ref.at[me, mine], z_send.at[d], z_recv.at[t], {"tensor": o}))
     go(remote(unit_ref, w_ref.at[me], y_send.at[n_tensor - 1], y_recv.at[t], y_peer))
     go(remote(unit_ref, w_ref.at[me], c_send.at[0], c_recv.at[at(0, t)], c_peer))
-    locals_ = [pltpu.make_async_copy(unit_ref, w_ref.at[me], own_sem.at[1])]
+    slots, width = rows_ref.shape[-1], counts_ref.shape[-1]
+    lanes = table.shape[-1]
+    lower = lax.broadcasted_iota(jnp.int32, (width, width), 0) >= lax.broadcasted_iota(jnp.int32, (width, width), 1)
+    places = lax.broadcasted_iota(jnp.int32, (width, lanes), 1)
+    table[...] = jnp.zeros_like(table)
+    for m in range(3):
+        running = jnp.sum(jnp.where(lower, counts_ref[m], 0), axis=1, keepdims=True)
+        table[pl.ds(m, 1), pl.ds(0, slots)] = rows_ref[m]
+        table[pl.ds(3 + m, 1), :] = jnp.sum((running <= places).astype(jnp.int32), axis=0, keepdims=True)
+    for d, o in enumerate(others):
+        go(remote(table, tables_ref.at[t], t_send.at[d], t_recv.at[t], {"tensor": o}))
+    locals_ = [pltpu.make_async_copy(table, tables_ref.at[t], own_sem.at[1])]
     for i, ref in enumerate((tok_ref, cot_ref)):
         locals_.append(pltpu.make_async_copy(ref.at[chunk(t)], acts_ref.at[i, t], own_sem.at[2 + i]))
     for copy in locals_:
         copy.start()
 
-    share_acts(0)
     for d, o in enumerate(others):
         part = w_ref.at[at(f, o), mine]
         arrived(part, z_recv.at[o])
@@ -300,6 +334,7 @@
         go(remote(part, part, y_send.at[d], y_recv.at[o], y_peer))
         go(remote(part, part, x_send.at[d], x_recv.at[at(0, o)], x_peer))
         if d == 1:
+            share_acts(0)
             share_acts(1)
     for d, o in enumerate(others):
         part = w_ref.at[at(f_y, o), mine]
@@ -317,6 +352,7 @@
         for o in [t] + others:
             arrived(w_ref.at[at(ff, o)], c_recv.at[at(k, o)])
     for o in others:
+        arrived(tables_ref.at[o], t_recv.at[o])
         for i in range(2):
             arrived(acts_ref.at[i, o], a_recv.at[2 * o + i])
     for copy in locals_:
@@ -325,26 +361,32 @@
         copy.wait_send()
 
 
-def bring(n_fsdp, n_tensor, unit, tokens, cotangent):
+def bring(n_fsdp, n_tensor, blocks, tokens, cotangent, block_rows, col_counts):
     tok_count, feats = tokens.shape
-    anywhere = pl.BlockSpec(memory_space=pl.ANY)
+    side = blocks[0].shape[-1]
+    anywhere, vmem = pl.BlockSpec(memory_space=pl.ANY), pl.BlockSpec(memory_space=pltpu.VMEM)
     sem = pltpu.SemaphoreType.DMA
+    parts = [b.reshape(-1, side) for b in blocks]
+    unit_rows = 3 * parts[0].shape[0]
     return pl.pallas_call(
         functools.partial(bring_kernel, n_tensor),
         out_shape=(
-            jax.ShapeDtypeStruct((n_fsdp * n_tensor,) + unit.shape, unit.dtype),
+            jax.ShapeDtypeStruct((n_fsdp * n_tensor, unit_rows, side), tokens.dtype),
             jax.ShapeDtypeStruct((2, n_tensor, tok_count // n_tensor, feats), tokens.dtype),
+            jax.ShapeDtypeStruct((n_tensor, 8, 128), jnp.int32),
         ),
-        in_specs=[anywhere] * 3,
-        out_specs=(anywhere,) * 2,
+        in_specs=[anywhere] * 5 + [vmem] * 2,
+        out_specs=(anywhere,) * 3,
         scratch_shapes=[
+            pltpu.VMEM((8, 128), jnp.int32),
             sem((n_tensor - 1,)), sem((n_tensor,)), sem((2 * n_tensor - 2,)), sem((2 * n_tensor,)), sem((2 * n_tensor - 2,)),
-            sem((n_tensor,)), sem((n_tensor,)), sem((2 * n_tensor,)), sem((2 * n_tensor,)), sem((2 * n_tensor,)), sem((4,)),
+            sem((n_tensor,)), sem((n_tensor,)), sem((2 * n_tensor,)), sem((2 * n_tensor,)), sem((2 * n_tensor,)),
+            sem((n_tensor - 1,)), sem((n_tensor,)), sem((7,)),
         ],
         compiler_params=pltpu.CompilerParams(
-            collective_id=0, has_side_effects=True, vmem_limit_bytes=2 * 1024 * 1024
+            collective_id=0, has_side_effects=True, vmem_limit_bytes=56 * 1024 * 1024
         ),
-    )(unit, tokens, cotangent)
+    )(*parts, tokens, cotangent, block_rows, col_counts)
 
 
 def return_kernel(
@@ -383,6 +425,7 @@
             go(remote(y_ref.at[i, o], outs[i].at[mine], a_send.at[2 * d + i], a_recv.at[2 * t + i], {"tensor": o}))
 
     share_out(0)
+    share_out(1)
     locals_ = [pltpu.make_async_copy(y_ref.at[i, t], outs[i].at[mine], own_sem.at[i]) for i in range(2)]
     for copy in locals_:
         copy.start()
@@ -420,8 +463,6 @@
             parts = parts + ((z_buf, 0),)
         fill(z_out, slot, at(f, order[d]), *parts)
         go(remote(z_out.at[slot], z_buf.at[slot], z_send.at[slot], z_recv.at[slot], peer))
-        if slot == 0:
-            share_out(1)
     parts = near(3) + ((z_buf, 1), (z_buf, 2))
     arrived(z_buf.at[1], z_recv.at[1])
     arrived(z_buf.at[2], z_recv.at[2])

time: 119 us -> 112 us (0.941)
  local copies, waits for them, and re-layouts: 11 us -> 7.78 us
  other arithmetic: 2.14 us -> 0 us
    pallas_call x1, Pallas kernels: 56.6 us -> 45.5 us  [send_back(): pl.pallas_call(functools.partial(return_kernel, n_tensor), out_shape=(big...]
    pallas_call x1, Pallas kernels: 39 us -> 47.4 us  [bring(): pl.pallas_call(functools.partial(bring_kernel, n_tensor), out_shape=(jax....]
    unnamed x17 -> x11, local copies, waits for them, and re-layouts: 10.8 us -> 7.78 us
    pallas_call x1, Pallas kernels: 9.14 us -> 10.9 us  [run_blocks(): pl.pallas_call(functools.partial(block_pass, slots, width, shares), out_s...]
where the time goes in v5:
time: 112 us
  Pallas kernels  104 us (93%)
  local copies, waits for them, and re-layouts  7.78 us (7%)
    pallas_call x1, Pallas kernels, bring(): pl.pallas_call(functools.partial(bring_kernel, n_tensor), out_shape=(jax....  47.4 us
    pallas_call x1, Pallas kernels, send_back(): pl.pallas_call(functools.partial(return_kernel, n_tensor), out_shape=(big...  45.5 us
    pallas_call x1, Pallas kernels, run_blocks(): pl.pallas_call(functools.partial(block_pass, slots, width, shares), out_s...  10.9 us
    unnamed x11, local copies, waits for them, and re-layouts  7.78 us

profile of v5, /device:TPU:0, one launch (start us, length us, event | category | flops | bytes accessed | tf_op | source)
XLA Modules:
  0.0 112.2 jit_solution(4149359593421184951)
XLA Ops:
  0.6 47.4 %shard_map.110 = (bf16[16,1152,128]{2,1,0:T(8,128)(2,1)}, bf16[2,4,64,1024]{3,2,1,0:T(8,128)(2,1)}, s32[4,8,128]{2,1,0:T(8,128)}) custom-call(bf16[384,128]{1,0:T(8,128)(2,1)} %bitcast.3, bf16[384,128]{1,0:T(8,128)(2,1)} %bitcast.4, bf16[384,128]{1,0:T(8,128)(2,1)} %bitcast.5, bf16[256,1024]{1,0:T(8,128)(2,1)} %tok_ref.1, bf16[256,1024]{1,0:T(8,128)(2,1)} %cot_ref.1, ...), custom_call_target="tpu_custom_call" | custom-call | tf_op jit(solution)/shard_map/pallas_call | solution.py:371
  48.0 0.0 copy-start
  48.0 2.3 %copy-done = bf16[16,1152,128]{2,1,0:T(8,128)(2,1)S(1)} copy-done((bf16[16,1152,128]{2,1,0:T(8,128)(2,1)S(1)}, bf16[16,1152,128]{2,1,0:T(8,128)(2,1)}, u32[]{:S(2)}) %copy-start) | copy-done | bytes 4718616
  50.3 0.0 copy-start.1
  50.3 1.2 %copy-done.1 = bf16[2,4,64,1024]{3,2,1,0:T(8,128)(2,1)S(1)} copy-done((bf16[2,4,64,1024]{3,2,1,0:T(8,128)(2,1)S(1)}, bf16[2,4,64,1024]{3,2,1,0:T(8,128)(2,1)}, u32[]{:S(2)}) %copy-start.1) | copy-done | bytes 1048600
  51.6 0.0 copy-start.2
  51.6 0.7 copy-done.2
  52.3 10.9 %shard_map.111 = (bf16[2,4,64,1024]{3,2,1,0:T(8,128)(2,1)S(1)}, bf16[16,9,64,128]{3,2,1,0:T(8,128)(2,1)S(1)}, bf16[16,9,64,128]{3,2,1,0:T(8,128)(2,1)S(1)}) custom-call(s32[4,8,128]{2,1,0:T(8,128)S(1)} %copy-done.2, bf16[2,4,64,1024]{3,2,1,0:T(8,128)(2,1)S(1)} %copy-done.1, bf16[16,1152,128]{2,1,0:T(8,128)(2,1)S(1)} %copy-done), custom_call_target="tpu_custom_call" | custom-call | tf_op jit(solution)/shard_map/pallas_call | solution.py:218
  63.2 45.5 %shard_map.112 = (bf16[256,1024]{1,0:T(8,128)(2,1)S(1)}, bf16[256,1024]{1,0:T(8,128)(2,1)S(1)}, bf16[1,3,128,128]{3,2,1,0:T(8,128)(2,1)S(1)}, bf16[1,3,128,128]{...) custom-call(bf16[2,4,64,1024]{3,2,1,0:T(8,128)(2,1)S(1)} %get-tuple-element.14.y_ref, ...), custom_call_target="tpu_custom_call" | custom-call | tf_op jit(solution)/shard_map/pallas_call | solution.py:494
  108.7 0.8 copy.17
  109.4 0.8 copy.18
  110.2 0.6 copy.19
  110.9 0.6 copy.20
  111.5 0.6 copy.21
Async XLA Ops:
  48.0 2.3 %copy-start = (bf16[16,1152,128]{2,1,0:T(8,128)(2,1)S(1)}, bf16[16,1152,128]{2,1,0:T(8,128)(2,1)}, u32[]{:S(2)}) copy-start(bf16[16,1152,128]{2,1,0:T(8,128)(2,1)} %get-tuple-element.13.w_hbm) | copy-start | bytes 14155780
  50.3 1.2 %copy-start.1 = (bf16[2,4,64,1024]{3,2,1,0:T(8,128)(2,1)S(1)}, bf16[2,4,64,1024]{3,2,1,0:T(8,128)(2,1)}, u32[]{:S(2)}) copy-start(bf16[2,4,64,1024]{3,2,1,0:T(8,128)(2,1)} %get-tuple-element.12.acts_hbm) | copy-start | bytes 3145732
  51.6 0.7 copy-start.2

commit v6 on v3

--- a/solution.py
+++ b/solution.py
@@ -116,8 +116,19 @@
     return (layer_out, input_grad, gate_grad, up_grad, down_grad)
 
 
-def block_pass(slots, width, shares, meta_ref, acts_ref, w_ref, y_ref, left_ref, right_ref, gate, up, dhid, hid, dgate, dup, acc):
-    n_tensor, tok, feats = acts_ref.shape[1:]
+def block_pass(slots, width, shares, meta_ref, acts_hbm, w_hbm, y_ref, left_ref, right_ref, gate, up, dhid, hid, dgate, dup, acc, acts_ref, w_ref, acts_sem, w_sem):
+    n_tensor, tok, feats = acts_hbm.shape[1:]
+
+    def load(t, buf):
+        return [
+            pltpu.make_async_copy(w_hbm.at[share * n_tensor + t], w_ref.at[buf * shares + share], w_sem.at[buf, share])
+            for share in range(shares)
+        ]
+
+    acts_copy = pltpu.make_async_copy(acts_hbm, acts_ref, acts_sem)
+    acts_copy.start()
+    for copy in load(0, 0):
+        copy.start()
     side = w_ref.shape[-1]
     per_chunk = feats // side
     per_share = slots // shares
@@ -136,7 +147,7 @@
 
     def place(t, m, s):
         share, k = divmod(s, per_share)
-        return share * n_tensor + t, pl.ds((m * per_share + k) * side, side)
+        return lax.rem(t, 2) * shares + share, pl.ds((m * per_share + k) * side, side)
 
     def weight(t, m, s):
         unit, rows = place(t, m, s)
@@ -147,12 +158,21 @@
 
     plain, right_t = ((1,), (0,)), ((1,), (1,))
     acc[...] = jnp.zeros_like(acc)
+    acts_copy.wait()
 
     @pl.loop(0, n_tensor)
     def _(t):
         gate[...] = jnp.zeros_like(gate)
         up[...] = jnp.zeros_like(up)
         dhid[...] = jnp.zeros_like(dhid)
+        for copy in load(t, lax.rem(t, 2)):
+            copy.wait()
+
+        @pl.when(t + 1 < n_tensor)
+        def _():
+            for copy in load(t + 1, lax.rem(t + 1, 2)):
+                copy.start()
+
         for m, which, dims, into in ((0, 0, plain, gate), (1, 0, plain, up), (2, 1, right_t, dhid)):
             terms = [dot(act(which, row_of(t, m, s)), weight(t, m, s), dims) for s in range(slots)]
             for s in range(slots):
@@ -198,11 +218,17 @@
     return pl.pallas_call(
         functools.partial(block_pass, slots, width, shares),
         out_shape=(jax.ShapeDtypeStruct(acts.shape, acts.dtype), picked, picked),
-        in_specs=[pl.BlockSpec(memory_space=pltpu.SMEM), vmem, vmem],
+        in_specs=[pl.BlockSpec(memory_space=pltpu.SMEM)] + [pl.BlockSpec(memory_space=pl.ANY)] * 2,
         out_specs=(vmem, vmem, vmem),
         scratch_shapes=[pltpu.VMEM(cols, jnp.float32)] * 3
         + [pltpu.VMEM(cols, jnp.bfloat16)] * 3
-        + [pltpu.VMEM((2, n_tensor * feats // side, tok, side), jnp.float32)],
+        + [
+            pltpu.VMEM((2, n_tensor * feats // side, tok, side), jnp.float32),
+            pltpu.VMEM(acts.shape, acts.dtype),
+            pltpu.VMEM((2 * shares,) + weights.shape[1:], weights.dtype),
+            pltpu.SemaphoreType.DMA,
+            pltpu.SemaphoreType.DMA((2, shares)),
+        ],
         compiler_params=pltpu.CompilerParams(vmem_limit_bytes=48 * 1024 * 1024),
     )(meta, acts, weights)
 
@@ -457,7 +483,7 @@
             sem((2 * n_tensor,)), sem((n_tensor,)), sem((n_tensor - 1,)), sem((2 * n_tensor,)), sem((3,)),
         ],
         compiler_params=pltpu.CompilerParams(
-            collective_id=1, has_side_effects=True, vmem_limit_bytes=40 * 1024 * 1024
+            collective_id=1, has_side_effects=True, vmem_limit_bytes=24 * 1024 * 1024
         ),
     )(y, lefts, rights)
 

time: 110 us -> 109 us (level)
  no operation moved by 1% of the time
where the time goes in v6:
time: 109 us
  Pallas kernels  97.3 us (89%)
  local copies, waits for them, and re-layouts  8.04 us (7%)
  other arithmetic  2.86 us (3%)
    pallas_call x1, Pallas kernels, send_back(): pl.pallas_call(functools.partial(return_kernel, n_tensor), out_shape=(big...  47.9 us
    pallas_call x1, Pallas kernels, bring(): pl.pallas_call(functools.partial(bring_kernel, n_tensor), out_shape=(jax....  37.7 us
    pallas_call x1, Pallas kernels, run_blocks(): pl.pallas_call(functools.partial(block_pass, slots, width, shares), out_s...  11.8 us
    unnamed x13, local copies, waits for them, and re-layouts  7.86 us

profile of v6, /device:TPU:0, one launch (start us, length us, event | category | flops | bytes accessed | tf_op | source)
XLA Modules:
  0.0 108.9 jit_solution(14317948703786999825)
XLA Ops:
  0.6 0.7 convert.13
  1.3 0.7 copy.19
  2.0 0.2 reduce_window_sum.14
  2.2 0.1 convert_reduce_fusion
  2.4 0.1 pad_maximum_fusion.1
  2.4 0.1 reshape.28
  2.5 1.7 %pad_maximum_fusion.unit_ref = bf16[1184,128]{1,0:T(8,128)(2,1)} fusion(bf16[32,128]{1,0:T(8,128)(2,1)S(1)} %pad_bitcast_fusion, bf16[384,128]{1,0:T(8,128)(2,1)} %bitcast.16, bf16[384,128]{1,0:T(8,128)(2,1)} %bitcast.17, bf16[384,128]{1,0:T(8,128)(2,1)} %bitcast.18), kind=kLoop, calls=%fused_computation | loop fusion | flops 1212416 | bytes 606208 | tf_op jit(solution)/shard_map/concatenate | solution.py:243
  4.3 37.7 %shard_map.110 = (bf16[16,1184,128]{2,1,0:T(8,128)(2,1)}, bf16[2,4,64,1024]{3,2,1,0:T(8,128)(2,1)}) custom-call(bf16[1184,128]{1,0:T(8,128)(2,1)} %pad_maximum_fusion.unit_ref, bf16[256,1024]{1,0:T(8,128)(2,1)} %tok_ref.1, bf16[256,1024]{1,0:T(8,128)(2,1)} %cot_ref.1), custom_call_target="tpu_custom_call" | custom-call | tf_op jit(solution)/shard_map/pallas_call | solution.py:360
  41.9 0.8 slice_bitcast_fusion
  42.7 0.1 reshape.33.meta_ref
  42.8 0.0 copy-start.1
  42.8 1.2 %copy-done.1 = bf16[2,4,64,1024]{3,2,1,0:T(8,128)(2,1)S(1)} copy-done((bf16[2,4,64,1024]{3,2,1,0:T(8,128)(2,1)S(1)}, bf16[2,4,64,1024]{3,2,1,0:T(8,128)(2,1)}, u32[]{:S(2)}) %copy-start.1) | copy-done | bytes 1048600
  44.0 11.8 %shard_map.111 = (bf16[2,4,64,1024]{3,2,1,0:T(8,128)(2,1)S(1)}, bf16[16,9,64,128]{3,2,1,0:T(8,128)(2,1)S(1)}, bf16[16,9,64,128]{3,2,1,0:T(8,128)(2,1)}) custom-call(s32[288]{0:T(512)S(1)} %reshape.33.meta_ref, bf16[2,4,64,1024]{3,2,1,0:T(8,128)(2,1)S(1)} %copy-done.1, bf16[16,1184,128]{2,1,0:T(8,128)(2,1)} %get-tuple-element.10.w_hbm), custom_call_target="tpu_custom_call" | custom-call | tf_op jit(solution)/shard_map/pallas_call | solution.py:218
  55.9 0.0 copy-start
  55.9 1.7 %copy-done = bf16[16,9,64,128]{3,2,1,0:T(8,128)(2,1)S(1)} copy-done((bf16[16,9,64,128]{3,2,1,0:T(8,128)(2,1)S(1)}, bf16[16,9,64,128]{3,2,1,0:T(8,128)(2,1)}, u32[]{:S(2)}) %copy-start) | copy-done | bytes 2359320
  57.5 47.9 %shard_map.112 = (bf16[256,1024]{1,0:T(8,128)(2,1)S(1)}, bf16[256,1024]{1,0:T(8,128)(2,1)S(1)}, bf16[1,3,128,128]{3,2,1,0:T(8,128)(2,1)S(1)}, bf16[1,3,128,128]{...) custom-call(bf16[2,4,64,1024]{3,2,1,0:T(8,128)(2,1)S(1)} %get-tuple-element.12.y_ref, ...), custom_call_target="tpu_custom_call" | custom-call | tf_op jit(solution)/shard_map/pallas_call | solution.py:475
  105.4 0.8 copy.26
  106.2 0.8 copy.27
  107.0 0.6 copy.28
  107.7 0.6 copy.29
  108.3 0.6 copy.30
  (5 shorter events, 0.0 us)
Async XLA Ops:
  42.8 1.2 %copy-start.1 = (bf16[2,4,64,1024]{3,2,1,0:T(8,128)(2,1)S(1)}, bf16[2,4,64,1024]{3,2,1,0:T(8,128)(2,1)}, u32[]{:S(2)}) copy-start(bf16[2,4,64,1024]{3,2,1,0:T(8,128)(2,1)} %get-tuple-element.11.acts_hbm) | copy-start | bytes 3145732
  55.9 1.7 %copy-start = (bf16[16,9,64,128]{3,2,1,0:T(8,128)(2,1)S(1)}, bf16[16,9,64,128]{3,2,1,0:T(8,128)(2,1)}, u32[]{:S(2)}) copy-start(bf16[16,9,64,128]{3,2,1,0:T(8,128)(2,1)} %get-tuple-element.14.right_ref) | copy-start | bytes 7077892
